TPU v7x, 128 devices: a whole 4x4x4 slice. The times are simulated.
128 devices in a mesh: cplx: 4 (over y), frag: 32 (over z, x, core).
Axes of the slice: x: 4, y: 4, z: 4, core: 2. Of those that a mesh axis runs over, the one named last changes fastest.
Arguments:
- coeffs: float32 [2048, 256], P(('cplx', 'frag')), parts along dimension 0, may hold values from -0.3 to 0.3
- centres: float32 [2048, 4, 256], P(('cplx', 'frag')), parts along dimension 0, may hold values from -3 to 3, as said below
- frag_sizes: int32 [2048], P(('cplx', 'frag')), parts along dimension 0, may hold values from 64 to 256
- pairs: int32 [131072, 2], P(('cplx', 'frag')), parts along dimension 0, may hold values from 0 to 511, as said below
Outputs:
- potential: float32 [2048, 256], P(('cplx', 'frag')), parts along dimension 0
There are 4 independent parts, one for each index of `cplx`. A program takes and returns all parts, laid end to end along the dimension named above; each array names one. Nothing has to cross between parts.
Inputs may be any that keep to these rules, and one draw needn't show every extreme that they name: `pairs`: slots 1024 * d to 1024 * (d + 1) - 1 belong to device d of frag; their first fragment is one of fragments 16 * d to 16 * (d + 1) - 1. Slot r of that block (counted from the block's start) either has its second fragment equal to its first (an empty slot) or names a second fragment owned by device r // 32, that is one of fragments 16 * (r // 32) on. Slots toward the device itself are never empty and never name the same fragment twice. `centres`: widths are positive.
All inputs are finite; a program needn't handle non-finite values.
Results may differ from a plain program's by a relative error of at most 0.0003.
Values sent between devices are 32-bit elements; how exact they have to be, the bound alone decides.
No kernel may reach another device: no remote copies, remote signals or barrier semaphores. Data moves between devices by JAX's collectives and lax.ppermute only.
A program may use at most 128 MiB of HBM per device.

v0:
```python
import functools

import jax
import jax.numpy as jnp
from jax import lax
from jax.experimental import pallas as pl
from jax.experimental.pallas import tpu as pltpu
from jax.sharding import PartitionSpec as P

FRAG_DEV = 16
AUX = 256
ROWS = 96
NF = 64
NG = 128
CHUNK = 32
CPF = AUX // CHUNK
WIDE = 4
NARROW = 8
SPAN = 64
DUMMY = NF * CPF
DEPTH = 48
COL = 24
UNROLL = 16
WIDTH_FLOOR = 1.0 / 32.0


def pieces(value):
    first = value.astype(jnp.bfloat16).astype(jnp.float32)
    rest = value - first
    second = rest.astype(jnp.bfloat16).astype(jnp.float32)
    return first, second, rest - second


def pair_kernel(meta, *refs):
    packets = refs[:11]
    out_sib, out_far, out_near, out_own, outf_far, outf_near, outf_own = refs[11:18]
    (lhs, rows_f, cols_f, rhs, build, slots, counts, chunks, zeros_v, places, ends,
     table_v, tiles_v, table, tile_list, sem) = refs[18:]
    f_blocks = [packets[0], packets[1], packets[2], packets[3]]
    g_blocks = [packets[0]] + list(packets[4:])
    plane = meta[0]
    column = meta[1]

    def put_rows(r, value):
        for h in range(2):
            build[h, pl.ds(r * 16, 16), :] = value[:, 128 * h:128 * h + 128]

    def take_rows(h, at, count):
        return build.at[h][pl.ds(at, count, stride=16), :]

    lowest = None
    for i, blk in enumerate(f_blocks):
        x, y, z, w, c = (blk[pl.ds(16 * k, 16), :] for k in range(5))
        lowest = w if lowest is None else jnp.minimum(lowest, w)
        s = x * x + y * y + z * z + w
        one = jnp.ones_like(x)
        zero = jnp.zeros_like(x)
        px, py, pz = pieces(-2.0 * x), pieces(-2.0 * y), pieces(-2.0 * z)
        ps, pw, pc = pieces(s), pieces(w), pieces(c)
        for k in range(3):
            delta = one if k == 0 else zero
            extra = pc if k == 0 else (pw if k == 1 else (zero, zero, zero))
            rows = [px[k], py[k], pz[k], delta, ps[k], *extra,
                    px[k], py[k], pz[k], delta, px[k], py[k], pz[k], delta]
            for r, value in enumerate(rows):
                put_rows(16 * k + r, value)

        def one_row(lf, _, i=i):
            for h in range(2):
                feats = take_rows(h, lf, DEPTH).T
                feats = jnp.concatenate([feats, jnp.zeros((128, 128 - DEPTH), jnp.float32)], axis=1)
                lhs[pl.ds((i * 16 + lf) * CPF + 4 * h, 4)] = feats.astype(jnp.bfloat16).reshape(4, CHUNK, 128)
            return 0

        lax.fori_loop(0, 16, one_row, 0, unroll=4)
    spare_lane = lax.broadcasted_iota(jnp.int32, (CHUNK, 128), 1)
    lhs[DUMMY] = (spare_lane == 4).astype(jnp.float32).astype(jnp.bfloat16)

    pick = lax.broadcasted_iota(jnp.int32, (128, 128), 0)

    def spread(rows, lo, hi, scale):
        sel = jnp.where((pick >= lo) & (pick <= hi), scale, 0.0)
        return jnp.dot(rows, sel.astype(jnp.bfloat16), preferred_element_type=jnp.float32)

    def one_spread(f, _):
        value = spread(lhs[pl.ds(f * CPF, CPF)].reshape(AUX, 128), 5, 7, 1.0)
        rows_f[pl.ds(f * CPF, CPF), 0:CHUNK, :] = value.reshape(CPF, CHUNK, 128)
        rows_f[pl.ds(f * CPF, CPF), CHUNK:2 * CHUNK, :] = jnp.zeros((CPF, CHUNK, 128), jnp.float32)
        return 0

    lax.fori_loop(0, NF, one_spread, 0, unroll=4)
    rows_f[DUMMY] = jnp.zeros((2 * CHUNK, 128), jnp.float32)

    for j, blk in enumerate(g_blocks):
        x, y, z, w, c = (blk[pl.ds(16 * k, 16), :] for k in range(5))
        lowest = jnp.minimum(lowest, w)
        s = x * x + y * y + z * z + w
        one = jnp.ones_like(x)
        zero = jnp.zeros_like(x)
        px, py, pz, ps = pieces(x), pieces(y), pieces(z), pieces(s)
        rows = [px[0], py[0], pz[0], ps[0], one, zero, zero, zero,
                px[1], py[1], pz[1], ps[1], px[2], py[2], pz[2], ps[2]]
        for r, value in enumerate(rows):
            put_rows(r, value)

        def one_column(lg, _, j=j, blk=blk):
            start = pl.multiple_of((j * 16 + lg) * 16, 16)
            base = pl.multiple_of((j * 16 + lg) * COL, COL)
            cols_f[pl.ds(base, 16), :] = jnp.zeros((16, 128), jnp.float32)
            coef = blk[pl.ds(64 + lg, 1), :]
            for h in range(2):
                cols_f[pl.ds(base + 16 + h, 1), :] = coef[:, 128 * h:128 * h + 128]
            rhs[pl.ds(start, 16), :] = jnp.concatenate([take_rows(h, lg, 16) for h in range(2)], axis=1).astype(jnp.bfloat16)
            return 0

        lax.fori_loop(0, 16, one_column, 0, unroll=8)

    lane = lax.broadcasted_iota(jnp.int32, (8, AUX), 1)
    back = jnp.zeros((8, AUX), jnp.float32)
    for j, blk in enumerate(g_blocks):
        shift = lax.rem(32 * j - 32 * column + 256, 256)
        turned = pltpu.roll(blk[pl.ds(80, 8), :], shift, 1)
        back = jnp.where(lane // 32 == j, turned, back)
    slots[...] = back
    g_lane = lax.broadcasted_iota(jnp.int32, (16, AUX), 0).astype(jnp.float32)
    g_ids = jnp.concatenate([g_lane + (16 * meta[8 + j]).astype(jnp.float32) for j in range(8)], axis=0)
    for i, blk in enumerate(f_blocks):
        f_ids = g_lane + (16 * meta[4 + i]).astype(jnp.float32)
        f_plane = meta[16 + i]

        def table_of(row_f, row_g):
            odd = (row_f + row_g) - 2.0 * jnp.floor((row_f + row_g) * 0.5)
            less = (row_f < row_g).astype(jnp.float32)
            use = (odd == less) & (row_f != row_g)
            row_f = jnp.where(use, row_f, -1.0)
            left = (row_f == f_ids).astype(jnp.float32).astype(jnp.bfloat16)
            right = (row_g == g_ids).astype(jnp.float32).astype(jnp.bfloat16)
            return lax.dot_general(left, right, (((1,), (1,)), ((), ())), preferred_element_type=jnp.float32)

        there = table_of(blk[pl.ds(80 + plane, 1), :], blk[pl.ds(84 + plane, 1), :])
        back_i = table_of(slots[pl.ds(4 + f_plane, 1), :], slots[pl.ds(f_plane, 1), :])
        counts[pl.ds(16 * i, 16), :] = there + back_i
        sizes = blk[pl.ds(88, 1), :]
        eye = lax.broadcasted_iota(jnp.int32, (16, AUX), 0) == lax.broadcasted_iota(jnp.int32, (16, AUX), 1)
        size_col = jnp.sum(jnp.where(eye, sizes, 0.0), axis=1, keepdims=True)
        many = jnp.floor((size_col + (CHUNK - 1)) * (1.0 / CHUNK))
        chunks[pl.ds(16 * i, 16), :] = jnp.broadcast_to(many, (16, 128))

    most = jnp.max(counts[...]).astype(jnp.int32)
    safe = jnp.min(lowest) >= WIDTH_FLOOR
    row8 = lax.broadcasted_iota(jnp.int32, (8, 128), 0)

    lane8 = lax.broadcasted_iota(jnp.int32, (8, 128), 1)
    sizes = jnp.zeros((8, 128), jnp.float32)
    for j, blk in enumerate(g_blocks):
        part = blk[pl.ds(88, 8), 0:128]
        part = part if j == 0 else pltpu.roll(part, 16 * j, 1)
        sizes = jnp.where(lane8 // 16 == j, part, sizes)
    slots[:, 0:128] = sizes
    is_wide = jnp.where(jnp.broadcast_to(slots[pl.ds(0, 1), 0:128], (8, 128)) > 128.0, 1.0, 0.0)
    per_tile = jnp.where(is_wide > 0.0, float(WIDE), float(NARROW))
    contract = (((1,), (1,)), ((), ()))

    def step(code, kind):
        take = NARROW if kind == "narrow" else WIDE
        g, q = code & 127, code >> 7
        at = [table[q + u // WIDE, u % WIDE, g] for u in range(take)]
        times = (at[0] >> 10).astype(jnp.float32)
        at = [e & 1023 if u % WIDE == 0 else e for u, e in enumerate(at)]
        base = pl.multiple_of(g * COL, COL)
        block = rhs[pl.ds(pl.multiple_of(g * 16, 16), 16), :]
        blank = jnp.zeros((128 - DEPTH, AUX), jnp.bfloat16)
        if kind == "narrow":
            left = jnp.concatenate(
                [jnp.concatenate([lhs[e] for e in at[:4]], axis=0), jnp.concatenate([lhs[e] for e in at[4:]], axis=0)], axis=1)
            thin = block[:, :128]
            none = jnp.zeros((128, 128), jnp.bfloat16)
            right = jnp.concatenate([thin, thin, thin, blank[:, :128]], axis=0)
            right = jnp.concatenate([jnp.concatenate([right, none], axis=1), jnp.concatenate([none, right], axis=1)], axis=0)
            kern = lax.rsqrt(jnp.dot(left, right, preferred_element_type=jnp.float32))
            ka, kb = kern[:, :128], kern[:, 128:]
            coef_a = jnp.concatenate([rows_f[e, 0:CHUNK, :] for e in at[:4]], axis=0)
            coef_b = jnp.concatenate([rows_f[e, 0:CHUNK, :] for e in at[4:]], axis=0)
            sec = jnp.sum((ka * coef_a + kb * coef_b).reshape(-1, 8, 128), axis=0)
            cols_f[pl.ds(base, 8), :] = cols_f[pl.ds(base, 8), :] + sec * times
            weight = cols_f[pl.ds(base + 16, 1), :] * times
            sums = [rows_f[e, CHUNK:2 * CHUNK, :] for e in at]
            first = [k[u * CHUNK:(u + 1) * CHUNK] * weight for k in (ka, kb) for u in range(4)]
        else:
            left = jnp.concatenate([lhs[e] for e in at], axis=0)
            if kind == "exact":
                part = block.astype(jnp.float32)
                dist = None
                for k in range(3):
                    mine = jnp.where(((pick % 16 == k) & (pick < DEPTH)), -0.5, 0.0).astype(jnp.bfloat16)
                    mine = jnp.dot(left, mine, preferred_element_type=jnp.float32)
                    other = part[k:k + 1] + part[8 + k:9 + k] + part[12 + k:13 + k]
                    gap = jnp.concatenate([mine, mine], axis=1) - other
                    dist = gap * gap if dist is None else dist + gap * gap
                wide = spread(left, 21, 23, 1.0)
                dist = dist + jnp.concatenate([wide, wide], axis=1) + width_row(g)
            else:
                right = jnp.concatenate([block, block, block, blank], axis=0)
                dist = jnp.dot(left, right, preferred_element_type=jnp.float32)
            kern = lax.rsqrt(dist)
            k0, k1 = kern[:, :128], kern[:, 128:]
            coef = jnp.concatenate([rows_f[e, 0:CHUNK, :] for e in at], axis=0)
            sec0 = jnp.sum((k0 * coef).reshape(-1, 8, 128), axis=0)
            sec1 = jnp.sum((k1 * coef).reshape(-1, 8, 128), axis=0)
            cols_f[pl.ds(base, 8), :] = cols_f[pl.ds(base, 8), :] + sec0 * times
            cols_f[pl.ds(base + 8, 8), :] = cols_f[pl.ds(base + 8, 8), :] + sec1 * times
            both = k0 * (cols_f[pl.ds(base + 16, 1), :] * times) + k1 * (cols_f[pl.ds(base + 17, 1), :] * times)
            sums = [rows_f[e, CHUNK:2 * CHUNK, :] for e in at]
            first = [both[u * CHUNK:(u + 1) * CHUNK] for u in range(take)]
        for e, value, more in zip(at, sums, first):
            rows_f[e, CHUNK:2 * CHUNK, :] = value + more

    def width_row(g):
        row = jnp.zeros((1, AUX), jnp.float32)
        for k, blk in enumerate(g_blocks):
            row = jnp.where(g // 16 == k, blk[pl.ds(48 + g % 16, 1), :], row)
        return row

    def one_round(state):
        r, _ = state
        groups = SPAN // 8
        at = [(row8 + 8 * t + SPAN * r).astype(jnp.float32) for t in range(groups)]

        def one_class(m, state):
            vals, times, total = state
            times = tuple(jnp.where(a >= total, m.astype(jnp.float32), v) for a, v in zip(at, times))

            def scan(f, state):
                vals, total = state
                many = jnp.broadcast_to(chunks[pl.ds(f, 1), :], (8, 128))
                listed = jnp.broadcast_to(counts[pl.ds(f, 1), :], (8, 128))
                mark = (many + f.astype(jnp.float32) * 16.0) * 4096.0 + total
                vals = tuple(jnp.where(a >= total, mark, v) for a, v in zip(at, vals))
                return vals, total + jnp.where(listed == m.astype(jnp.float32), many, 0.0)

            vals, total = lax.fori_loop(0, NF, scan, (vals, total), unroll=8)
            vals = tuple(jnp.where(a >= total, -1.0, v) for a, v in zip(at, vals))
            total = jnp.floor((total + per_tile - 1.0) / per_tile) * per_tile
            return vals, times, total

        flat = zeros_v[...]
        none = (flat,) * groups
        vals, times, total = lax.fori_loop(1, most + 1, one_class, (none, none, flat))
        for t in range(groups):
            code = jnp.floor(vals[t] * (1.0 / 4096.0))
            offset = at[t] - (vals[t] - 4096.0 * code)
            frag = jnp.floor(code * (1.0 / 16.0))
            entry = jnp.where((vals[t] >= 0.0) & (at[t] < total), frag * CPF + offset, float(DUMMY))
            places[0, pl.ds(8 * t, 8), :] = entry
            places[1, pl.ds(8 * t, 8), :] = times[t]
        groups4 = SPAN // WIDE
        for u in range(WIDE):
            value = places.at[0][pl.ds(u, groups4, stride=WIDE), :]
            if u == 0:
                value = value + 1024.0 * places.at[1][pl.ds(u, groups4, stride=WIDE), :]
            table_v[pl.ds(0, groups4), u, :] = value.astype(jnp.int32)
        table_v[pl.ds(groups4, 2)] = jnp.full((2, WIDE, 128), DUMMY, jnp.int32)
        left_over = jnp.clip(total - (SPAN * r).astype(jnp.float32), 0.0, float(SPAN))
        tiles = left_over / per_tile
        tiles_wide = tiles * is_wide
        tiles_thin = tiles - tiles_wide
        for k, tiles in enumerate((tiles_wide, tiles_thin)):
            ends[k] = lax.dot_general(upto, jnp.concatenate([tiles] * 16, axis=0).astype(jnp.bfloat16), contract, preferred_element_type=jnp.float32)
        number = [(lane8 + 128 * row8 + 1024 * k).astype(jnp.float32) for k in range(2)]

        def seek(c, state):
            out = []
            column = (c + 1).astype(jnp.float32)
            for k, (where, begin) in enumerate(state):
                end = jnp.broadcast_to(ends.at[k // 2][pl.ds(c, 1), :], (8, 128))
                hit = number[k % 2] >= end
                out.append((jnp.where(hit, column, where), jnp.where(hit, end, begin)))
            return tuple(out)

        found = lax.fori_loop(0, NG, seek, ((flat, flat),) * 3, unroll=8)
        for k, (where, begin) in enumerate(found):
            place = (number[k % 2] - begin) * (1.0 if k < 2 else 2.0) * 128.0 + where
            place = jnp.where(where < float(NG), place, float(groups4 * 128))
            tiles_v[pl.ds(8 * k, 8), :] = place.astype(jnp.int32)
        info = jnp.where(row8 == 0, jnp.sum(tiles_wide, axis=1, keepdims=True), jnp.sum(tiles_thin, axis=1, keepdims=True))
        tiles_v[pl.ds(24, 8), :] = info.astype(jnp.int32)
        longest = jnp.max(total).astype(jnp.int32)
        copies = [pltpu.make_async_copy(table_v, table, sem.at[0]), pltpu.make_async_copy(tiles_v, tile_list, sem.at[1])]
        for copy in copies:
            copy.start()
        for copy in copies:
            copy.wait()
        count_wide, count_thin = tile_list[24, 0], tile_list[25, 0]

        def many_tiles(kind, first_row, count):
            def body(i, _):
                row, col = first_row + (i >> 3), (i & 7) * UNROLL
                for u in range(UNROLL):
                    step(tile_list[row, col + u], kind)
                return 0

            lax.fori_loop(0, (count + (UNROLL - 1)) // UNROLL, body, 0)

        @pl.when(safe)
        def _():
            many_tiles("wide", 0, count_wide)
            many_tiles("narrow", 16, count_thin)

        @pl.when(jnp.logical_not(safe))
        def _():
            def wide_one(t, _):
                step(tile_list[t >> 7, t & 127], "exact")
                return 0

            def thin_one(t, _):
                step(tile_list[16 + (t >> 8), (t & 255) >> 1] + 128 * (t & 1), "exact")
                return 0

            lax.fori_loop(0, count_wide, wide_one, 0)
            lax.fori_loop(0, 2 * count_thin, thin_one, 0)

        return r + 1, longest

    zeros_v[...] = jnp.zeros_like(zeros_v)
    upto = (lax.broadcasted_iota(jnp.int32, (128, 128), 1) <= pick).astype(jnp.float32).astype(jnp.bfloat16)
    lax.while_loop(lambda state: state[0] * SPAN < state[1], one_round, (jnp.int32(0), jnp.int32(1)))

    lanes = lax.broadcasted_iota(jnp.int32, (AUX, 128), 1)

    def collect(f, out):
        col = jnp.sum(rows_f[pl.ds(f * CPF, CPF), CHUNK:2 * CHUNK, :].reshape(AUX, 128), axis=1, keepdims=True)
        return jnp.where(lanes == f, col, out)

    rows_out = rows_f[pl.ds(0, CPF), 0:CHUNK, :].reshape(AUX, 128)
    rows_out = lax.fori_loop(0, NF, collect, rows_out).T
    outf_own[...] = rows_out[0:16]
    outf_near[...] = rows_out[16:32]
    outf_far[...] = rows_out[32:64]
    cols = []
    for h in range(2):
        half = cols_f[pl.ds(8 * h, NG, stride=COL), :]
        for r in range(1, 8):
            half = half + cols_f[pl.ds(8 * h + r, NG, stride=COL), :]
        cols.append(half)
    cols = jnp.concatenate(cols, axis=1)
    out_own[...] = cols[0:16]
    out_near[...] = cols[16:32]
    out_far[...] = cols[32:64]
    out_sib[...] = cols[64:128]


def rectangle(meta, packets):
    vmem = pl.BlockSpec(memory_space=pltpu.VMEM)
    shape = lambda rows: jax.ShapeDtypeStruct((rows, AUX), jnp.float32)
    return pl.pallas_call(
        pair_kernel,
        out_shape=(shape(64), shape(32), shape(16), shape(16), shape(32), shape(16), shape(16)),
        in_specs=[pl.BlockSpec(memory_space=pltpu.SMEM)] + [vmem] * 11,
        out_specs=(vmem,) * 7,
        scratch_shapes=[
            pltpu.VMEM((DUMMY + 1, CHUNK, 128), jnp.bfloat16),
            pltpu.VMEM((DUMMY + 1, 2 * CHUNK, 128), jnp.float32),
            pltpu.VMEM((NG * COL, 128), jnp.float32),
            pltpu.VMEM((NG * 16, AUX), jnp.bfloat16),
            pltpu.VMEM((2, DEPTH * 16, 128), jnp.float32),
            pltpu.VMEM((8, AUX), jnp.float32),
            pltpu.VMEM((NF, 128), jnp.float32),
            pltpu.VMEM((NF, 128), jnp.float32),
            pltpu.VMEM((8, 128), jnp.float32),
            pltpu.VMEM((2, SPAN, 128), jnp.float32),
            pltpu.VMEM((2, 128, 128), jnp.float32),
            pltpu.VMEM((SPAN // WIDE + 2, WIDE, 128), jnp.int32),
            pltpu.VMEM((32, 128), jnp.int32),
            pltpu.SMEM((SPAN // WIDE + 2, WIDE, 128), jnp.int32),
            pltpu.SMEM((32, 128), jnp.int32),
            pltpu.SemaphoreType.DMA((2,)),
        ],
        compiler_params=pltpu.CompilerParams(vmem_limit_bytes=56 * 2**20),
    )(meta, *packets)


def index_of(z, x, c):
    return (z * 4 + x) * 2 + c


def partners(move):
    return [
        (index_of(z, x, c), index_of(*move(z, x, c)))
        for z in range(4) for x in range(4) for c in range(2)
    ]


X_NEAR = partners(lambda z, x, c: (z, x ^ 1, c))
X_FAR = partners(lambda z, x, c: (z, 3 - x, c))
Z_NEAR = partners(lambda z, x, c: (z ^ 1, x, c))
Z_FAR = partners(lambda z, x, c: (3 - z, x, c))
CORE = partners(lambda z, x, c: (z, x, c ^ 1))


def swap(array, pairs):
    return lax.ppermute(array, "frag", pairs)


def local(coeffs, centres, frag_sizes, pairs):
    me = lax.axis_index("frag")
    z, x, c = me // 8, (me // 2) % 4, me % 2
    mask = (jnp.arange(AUX, dtype=jnp.int32)[None, :] < frag_sizes[:, None]).astype(jnp.float32)
    packet = jnp.concatenate(
        [
            centres.transpose(1, 0, 2).reshape(4 * FRAG_DEV, AUX),
            coeffs * mask,
            pairs.T.reshape(8, AUX).astype(jnp.float32),
            jnp.pad(frag_sizes.astype(jnp.float32)[None, :], ((0, 7), (0, AUX - FRAG_DEV))),
        ],
        axis=0,
    )
    zs = jnp.stack([z, z ^ 1, 3 - z, (3 - z) ^ 1])
    xs = jnp.stack([x, x ^ 1, 3 - x, (3 - x) ^ 1])
    f_dev = index_of(zs, x, c)
    g_dev = jnp.concatenate([index_of(z, xs, c), index_of(z, xs, c ^ 1)])
    zero = jnp.zeros((2,), jnp.int32)
    meta = jnp.concatenate([jnp.stack([z, 2 * x + c]), zero, f_dev, g_dev, zs]).astype(jnp.int32)

    x_near = swap(packet, X_NEAR)
    z_near = swap(packet, Z_NEAR)
    x_far = swap(packet, X_FAR)
    z_far = swap(packet, Z_FAR)
    x_last = swap(x_near, X_FAR)
    z_last = swap(z_near, Z_FAR)
    own_c = swap(packet, CORE)
    near_c = swap(x_near, CORE)
    far_c = swap(x_far, CORE)
    last_c = swap(x_last, CORE)

    g_sib, g_far, g_near, g_own, f_far, f_near, f_own = rectangle(
        meta,
        (packet, z_near, z_far, z_last, x_near, x_far, x_last, own_c, near_c, far_c, last_c),
    )
    f_back = swap(f_far, Z_FAR)
    sib_back = swap(g_sib, CORE)
    far_back = swap(g_far + sib_back[32:], X_FAR)
    f_last = swap(f_near + f_back[16:], Z_NEAR)
    near_back = swap(g_near + sib_back[16:32] + far_back[16:], X_NEAR)
    total = f_own + f_back[:16] + f_last + g_own + sib_back[:16] + far_back[:16] + near_back
    return total * mask


def solution(mesh):
    return jax.shard_map(
        local,
        mesh=mesh,
        in_specs=(
            P(("cplx", "frag"), None),
            P(("cplx", "frag"), None, None),
            P(("cplx", "frag")),
            P(("cplx", "frag"), None),
        ),
        out_specs=P(("cplx", "frag"), None),
        check_vma=False,
    )
```

profile of v0, /device:TPU:0, one launch (start us, length us, event | category | flops | bytes accessed | tf_op | source)
XLA Modules:
  0.0 252.0 jit_solution(14017617301577562460)
XLA Ops:
  0.0 0.7 convert_bitcast_fusion.1
  0.7 0.7 convert_bitcast_fusion
  1.4 0.8 fusion.4
  2.2 1.7 collective-permute-start.3
  3.9 2.1 collective-permute-start.4
  6.0 4.0 %collective-permute-start.1 = (f32[96,256]{1,0:T(8,128)S(1)}, f32[96,256]{1,0:T(8,128)S(1)}, u32[]{:S(2)}, u32[]{:S(2)}) collective-permute-start(f32[96,256]{1,0:T(8,128)S(1)} %select_maximum_fusion.refs_0_), channel_id=1, source_target_pairs={{0,24},{1,25},{2,26},{3,27},{4,28},{5,29},{6,30},{7,31},{8,16},{9,... | collective-permute-start | bytes 294920 | tf_op jit(solution)/shard_map/ppermute | solution.py:401
  10.0 1.2 collective-permute-start.5
  11.5 0.5 collective-permute-start.8
  12.0 2.7 %collective-permute-done.refs_1_ = f32[96,256]{1,0:T(8,128)S(1)} collective-permute-done((f32[96,256]{1,0:T(8,128)S(1)}, f32[96,256]{1,0:T(8,128)S(1)}, u32[]{:S(2)}, u32[]{:S(2)}) %collective-permute-start) | collective-permute-done | bytes 98336 | tf_op jit(solution)/shard_map/ppermute | solution.py:401
  14.7 0.3 collective-permute-start.2
  15.0 1.0 collective-permute-done.5.refs_6_
  16.1 0.6 concatenate.7.meta
  16.7 3.8 %collective-permute-done.2.refs_3_ = f32[96,256]{1,0:T(8,128)S(1)} collective-permute-done((f32[96,256]{1,0:T(8,128)S(1)}, f32[96,256]{1,0:T(8,128)S(1)}, u32[]{:S(2)}, u32[]{:S(2)}) %collective-permute-start.2) | collective-permute-done | bytes 98336 | tf_op jit(solution)/shard_map/ppermute | solution.py:401
  20.6 0.5 copy-done.9
  21.1 0.6 copy-done.10
  21.8 194.3 %shard_map.46 = (f32[64,256]{1,0:T(8,128)}, f32[32,256]{1,0:T(8,128)}, f32[16,256]{1,0:T(8,128)}, f32[16,256]{1,0:T(8,128)}, f32[32,256]{1,0:T(8,128)}, /*index=5*/f32[16,256]{1,0:T(8,128)}, f32[16,256]{1,0:T(8,128)}) custom-call(s32[20]{0:T(128)} %concatenate.7.meta, f32[96,256]{1,0:T(8,128)} %copy-done, f32[96,256]{1,0:T(8,128)} %copy-done.5, ...), custom_call_target="tpu_custom_call" | custom-call | tf_op jit(solution)/shard_map/pallas_call | solution.py:355
  216.2 7.0 %collective-permute-start.10 = (f32[32,256]{1,0:T(8,128)}, f32[32,256]{1,0:T(8,128)S(1)}, u32[]{:S(2)}, u32[]{:S(2)}) collective-permute-start(f32[32,256]{1,0:T(8,128)} %get-tuple-element.13), channel_id=1, source_target_pairs={{0,24},{1,25},{2,26},{3,27},{4,28},{5,29},{6,30},{7,31},{8,16},{9,... | collective-permute-start | bytes 98312 | tf_op jit(solution)/shard_map/ppermute | solution.py:401
  223.2 0.8 slice_add_fusion
  223.9 11.1 %collective-permute-start.13 = (f32[32,256]{1,0:T(8,128)S(1)}, f32[32,256]{1,0:T(8,128)S(1)}, u32[]{:S(2)}, u32[]{:S(2)}) collective-permute-start(f32[32,256]{1,0:T(8,128)S(1)} %slice_add_fusion), channel_id=1, source_target_pairs={{0,6},{1,7},{2,4},{3,5},{4,2},{5,3},{6,0},{7,1},{8,14},{9,15},{10,... | collective-permute-start | bytes 98312 | tf_op jit(solution)/shard_map/ppermute | solution.py:401
  235.0 11.8 %collective-permute-start.11 = (f32[16,256]{1,0:T(8,128)S(1)}, f32[16,256]{1,0:T(8,128)S(1)}, u32[]{:S(2)}, u32[]{:S(2)}) collective-permute-start(f32[16,256]{1,0:T(8,128)S(1)} %slice_add_fusion.5), channel_id=1, source_target_pairs={{0,8},{1,9},{2,10},{3,11},{4,12},{5,13},{6,14},{7,15},{8,0},{9,1},... | collective-permute-start | bytes 49160 | tf_op jit(solution)/shard_map/ppermute | solution.py:401
  246.9 1.6 collective-permute-done.11
  248.5 2.1 collective-permute-done.14
  250.7 0.6 copy-done.16
  251.3 0.7 fusion.1
  (55 shorter events, 0.6 us)
Async XLA Ops:
  2.2 18.3 %copy-start = (f32[96,256]{1,0:T(8,128)}, f32[96,256]{1,0:T(8,128)S(1)}, u32[]{:S(2)}) copy-start(f32[96,256]{1,0:T(8,128)S(1)} %select_maximum_fusion.refs_0_) | copy-start | bytes 294916
  2.2 7.8 %collective-permute-start.3 = (f32[96,256]{1,0:T(8,128)S(1)}, f32[96,256]{1,0:T(8,128)S(1)}, u32[]{:S(2)}, u32[]{:S(2)}) collective-permute-start(f32[96,256]{1,0:T(8,128)S(1)} %select_maximum_fusion.refs_0_), channel_id=1, source_target_pairs={{0,2},{1,3},{2,0},{3,1},{4,6},{5,7},{6,4},{7,5},{8,10},{9,11},{10,... | collective-permute-start | bytes 294920 | tf_op jit(solution)/shard_map/ppermute | solution.py:401
  3.9 7.5 %collective-permute-start.6 = (f32[96,256]{1,0:T(8,128)S(1)}, f32[96,256]{1,0:T(8,128)S(1)}, u32[]{:S(2)}, u32[]{:S(2)}) collective-permute-start(f32[96,256]{1,0:T(8,128)S(1)} %select_maximum_fusion.refs_0_), channel_id=1, source_target_pairs={{0,1},{1,0},{2,3},{3,2},{4,5},{5,4},{6,7},{7,6},{8,9},{9,8},{10,11... | collective-permute-start | bytes 294920 | tf_op jit(solution)/shard_map/ppermute | solution.py:401
  3.9 7.5 %collective-permute-start.4 = (f32[96,256]{1,0:T(8,128)S(1)}, f32[96,256]{1,0:T(8,128)S(1)}, u32[]{:S(2)}, u32[]{:S(2)}) collective-permute-start(f32[96,256]{1,0:T(8,128)S(1)} %select_maximum_fusion.refs_0_), channel_id=1, source_target_pairs={{0,6},{1,7},{2,4},{3,5},{4,2},{5,3},{6,0},{7,1},{8,14},{9,15},{10,... | collective-permute-start | bytes 294920 | tf_op jit(solution)/shard_map/ppermute | solution.py:401
  6.0 10.7 %collective-permute-start.1 = (f32[96,256]{1,0:T(8,128)S(1)}, f32[96,256]{1,0:T(8,128)S(1)}, u32[]{:S(2)}, u32[]{:S(2)}) collective-permute-start(f32[96,256]{1,0:T(8,128)S(1)} %select_maximum_fusion.refs_0_), channel_id=1, source_target_pairs={{0,24},{1,25},{2,26},{3,27},{4,28},{5,29},{6,30},{7,31},{8,16},{9,... | collective-permute-start | bytes 294920 | tf_op jit(solution)/shard_map/ppermute | solution.py:401
  10.0 4.6 %collective-permute-start = (f32[96,256]{1,0:T(8,128)S(1)}, f32[96,256]{1,0:T(8,128)S(1)}, u32[]{:S(2)}, u32[]{:S(2)}) collective-permute-start(f32[96,256]{1,0:T(8,128)S(1)} %select_maximum_fusion.refs_0_), channel_id=1, source_target_pairs={{0,8},{1,9},{2,10},{3,11},{4,12},{5,13},{6,14},{7,15},{8,0},{9,1},... | collective-permute-start | bytes 294920 | tf_op jit(solution)/shard_map/ppermute | solution.py:401
  10.0 10.5 %copy-start.1 = (f32[96,256]{1,0:T(8,128)}, f32[96,256]{1,0:T(8,128)S(1)}, u32[]{:S(2)}) copy-start(f32[96,256]{1,0:T(8,128)S(1)} %collective-permute-done.3.refs_4_) | copy-start | bytes 294916
  10.0 5.9 %collective-permute-start.5 = (f32[96,256]{1,0:T(8,128)S(1)}, f32[96,256]{1,0:T(8,128)S(1)}, u32[]{:S(2)}, u32[]{:S(2)}) collective-permute-start(f32[96,256]{1,0:T(8,128)S(1)} %collective-permute-done.3.refs_4_), channel_id=1, source_target_pairs={{0,6},{1,7},{2,4},{3,5},{4,2},{5,3},{6,0},{7,1},{8,14},{9,15},{10,... | collective-permute-start | bytes 294920 | tf_op jit(solution)/shard_map/ppermute | solution.py:401
  11.4 9.2 %copy-start.2 = (f32[96,256]{1,0:T(8,128)}, f32[96,256]{1,0:T(8,128)S(1)}, u32[]{:S(2)}) copy-start(f32[96,256]{1,0:T(8,128)S(1)} %collective-permute-done.6.refs_7_) | copy-start | bytes 294916
  11.4 5.4 %collective-permute-start.7 = (f32[96,256]{1,0:T(8,128)S(1)}, f32[96,256]{1,0:T(8,128)S(1)}, u32[]{:S(2)}, u32[]{:S(2)}) collective-permute-start(f32[96,256]{1,0:T(8,128)S(1)} %collective-permute-done.3.refs_4_), channel_id=1, source_target_pairs={{0,1},{1,0},{2,3},{3,2},{4,5},{5,4},{6,7},{7,6},{8,9},{9,8},{10,11... | collective-permute-start | bytes 294920 | tf_op jit(solution)/shard_map/ppermute | solution.py:401
  11.5 9.1 %copy-start.3 = (f32[96,256]{1,0:T(8,128)}, f32[96,256]{1,0:T(8,128)S(1)}, u32[]{:S(2)}) copy-start(f32[96,256]{1,0:T(8,128)S(1)} %collective-permute-done.4.refs_5_) | copy-start | bytes 294916
  11.5 5.2 %collective-permute-start.8 = (f32[96,256]{1,0:T(8,128)S(1)}, f32[96,256]{1,0:T(8,128)S(1)}, u32[]{:S(2)}, u32[]{:S(2)}) collective-permute-start(f32[96,256]{1,0:T(8,128)S(1)} %collective-permute-done.4.refs_5_), channel_id=1, source_target_pairs={{0,1},{1,0},{2,3},{3,2},{4,5},{5,4},{6,7},{7,6},{8,9},{9,8},{10,11... | collective-permute-start | bytes 294920 | tf_op jit(solution)/shard_map/ppermute | solution.py:401
  14.7 5.9 %copy-start.5 = (f32[96,256]{1,0:T(8,128)}, f32[96,256]{1,0:T(8,128)S(1)}, u32[]{:S(2)}) copy-start(f32[96,256]{1,0:T(8,128)S(1)} %collective-permute-done.refs_1_) | copy-start | bytes 294916
  14.7 5.8 %collective-permute-start.2 = (f32[96,256]{1,0:T(8,128)S(1)}, f32[96,256]{1,0:T(8,128)S(1)}, u32[]{:S(2)}, u32[]{:S(2)}) collective-permute-start(f32[96,256]{1,0:T(8,128)S(1)} %collective-permute-done.refs_1_), channel_id=1, source_target_pairs={{0,24},{1,25},{2,26},{3,27},{4,28},{5,29},{6,30},{7,31},{8,16},{9,... | collective-permute-start | bytes 294920 | tf_op jit(solution)/shard_map/ppermute | solution.py:401
  16.0 4.6 %copy-start.6 = (f32[96,256]{1,0:T(8,128)}, f32[96,256]{1,0:T(8,128)S(1)}, u32[]{:S(2)}) copy-start(f32[96,256]{1,0:T(8,128)S(1)} %collective-permute-done.5.refs_6_) | copy-start | bytes 294916
  16.0 4.5 %collective-permute-start.9 = (f32[96,256]{1,0:T(8,128)S(1)}, f32[96,256]{1,0:T(8,128)S(1)}, u32[]{:S(2)}, u32[]{:S(2)}) collective-permute-start(f32[96,256]{1,0:T(8,128)S(1)} %collective-permute-done.5.refs_6_), channel_id=1, source_target_pairs={{0,1},{1,0},{2,3},{3,2},{4,5},{5,4},{6,7},{7,6},{8,9},{9,8},{10,11... | collective-permute-start | bytes 294920 | tf_op jit(solution)/shard_map/ppermute | solution.py:401
  16.7 3.9 %copy-start.8 = (f32[96,256]{1,0:T(8,128)}, f32[96,256]{1,0:T(8,128)S(1)}, u32[]{:S(2)}) copy-start(f32[96,256]{1,0:T(8,128)S(1)} %collective-permute-done.8.refs_9_) | copy-start | bytes 294916
  216.1 7.1 %collective-permute-start.12 = (f32[64,256]{1,0:T(8,128)}, f32[64,256]{1,0:T(8,128)S(1)}, u32[]{:S(2)}, u32[]{:S(2)}) collective-permute-start(f32[64,256]{1,0:T(8,128)} %get-tuple-element.16), channel_id=1, source_target_pairs={{0,1},{1,0},{2,3},{3,2},{4,5},{5,4},{6,7},{7,6},{8,9},{9,8},{10,11... | collective-permute-start | bytes 196616 | tf_op jit(solution)/shard_map/ppermute | solution.py:401
  216.2 18.8 %collective-permute-start.10 = (f32[32,256]{1,0:T(8,128)}, f32[32,256]{1,0:T(8,128)S(1)}, u32[]{:S(2)}, u32[]{:S(2)}) collective-permute-start(f32[32,256]{1,0:T(8,128)} %get-tuple-element.13), channel_id=1, source_target_pairs={{0,24},{1,25},{2,26},{3,27},{4,28},{5,29},{6,30},{7,31},{8,16},{9,... | collective-permute-start | bytes 98312 | tf_op jit(solution)/shard_map/ppermute | solution.py:401
  223.2 11.9 %copy-start.12 = (f32[16,256]{1,0:T(8,128)S(1)}, f32[16,256]{1,0:T(8,128)}, u32[]{:S(2)}) copy-start(f32[16,256]{1,0:T(8,128)} %get-tuple-element.14) | copy-start | bytes 49156
  223.9 22.9 %collective-permute-start.13 = (f32[32,256]{1,0:T(8,128)S(1)}, f32[32,256]{1,0:T(8,128)S(1)}, u32[]{:S(2)}, u32[]{:S(2)}) collective-permute-start(f32[32,256]{1,0:T(8,128)S(1)} %slice_add_fusion), channel_id=1, source_target_pairs={{0,6},{1,7},{2,4},{3,5},{4,2},{5,3},{6,0},{7,1},{8,14},{9,15},{10,... | collective-permute-start | bytes 98312 | tf_op jit(solution)/shard_map/ppermute | solution.py:401
  235.0 11.8 %copy-start.13 = (f32[16,256]{1,0:T(8,128)S(1)}, f32[16,256]{1,0:T(8,128)}, u32[]{:S(2)}) copy-start(f32[16,256]{1,0:T(8,128)} %get-tuple-element.18) | copy-start | bytes 49156
  235.0 13.5 %collective-permute-start.11 = (f32[16,256]{1,0:T(8,128)S(1)}, f32[16,256]{1,0:T(8,128)S(1)}, u32[]{:S(2)}, u32[]{:S(2)}) collective-permute-start(f32[16,256]{1,0:T(8,128)S(1)} %slice_add_fusion.5), channel_id=1, source_target_pairs={{0,8},{1,9},{2,10},{3,11},{4,12},{5,13},{6,14},{7,15},{8,0},{9,1},... | collective-permute-start | bytes 49160 | tf_op jit(solution)/shard_map/ppermute | solution.py:401
  246.9 3.8 %collective-permute-start.14 = (f32[16,256]{1,0:T(8,128)S(1)}, f32[16,256]{1,0:T(8,128)S(1)}, u32[]{:S(2)}, u32[]{:S(2)}) collective-permute-start(f32[16,256]{1,0:T(8,128)S(1)} %slice_add_fusion.1), channel_id=1, source_target_pairs={{0,2},{1,3},{2,0},{3,1},{4,6},{5,7},{6,4},{7,5},{8,10},{9,11},{10,... | collective-permute-start | bytes 49160 | tf_op jit(solution)/shard_map/ppermute | solution.py:401
  (8 other events, 19.6 us)
where the time goes:
time: 254 us; the launch traced here: 252 us
  Pallas kernels  194 us (76%)
  starting transfers between devices  39.9 us (16%)
  waiting for transfers between devices  11.3 us (4%)
  other arithmetic  3.82 us (2%)
    pallas_call x1, Pallas kernels, rectangle(): pl.pallas_call(pair_kernel, out_shape=(shape(64), shape(32), shape(16), s...  194 us
    ppermute x15, starting transfers between devices, swap(): return lax.ppermute(array, 'frag', pairs)  39.9 us
    ppermute x15, waiting for transfers between devices, swap(): return lax.ppermute(array, 'frag', pairs)  11.3 us
  transfers between devices with their start and end apart: 15, of which 5 were waited for; matrix products, arithmetic and copies ran while one was open for 1% of the time, Pallas kernels for 0%

commit v1 on v0

--- a/solution.py
+++ b/solution.py
@@ -19,8 +19,7 @@
 SPAN = 64
 DUMMY = NF * CPF
 DEPTH = 48
-COL = 24
-UNROLL = 16
+BATCH = 8
 WIDTH_FLOOR = 1.0 / 32.0
 
 
@@ -34,8 +33,8 @@
 def pair_kernel(meta, *refs):
     packets = refs[:11]
     out_sib, out_far, out_near, out_own, outf_far, outf_near, outf_own = refs[11:18]
-    (lhs, rows_f, cols_f, rhs, build, slots, counts, chunks, zeros_v, places, ends,
-     table_v, tiles_v, table, tile_list, sem) = refs[18:]
+    (lhs, rows_c, rows_s, cols_s, cols_c, rhs, build, slots, counts, chunks, zeros_v, places, ends,
+     table_v, tiles_v, dist_a, dist_b, table, tile_list, held_a, held_b, sem) = refs[18:]
     f_blocks = [packets[0], packets[1], packets[2], packets[3]]
     g_blocks = [packets[0]] + list(packets[4:])
     plane = meta[0]
@@ -84,12 +83,13 @@
 
     def one_spread(f, _):
         value = spread(lhs[pl.ds(f * CPF, CPF)].reshape(AUX, 128), 5, 7, 1.0)
-        rows_f[pl.ds(f * CPF, CPF), 0:CHUNK, :] = value.reshape(CPF, CHUNK, 128)
-        rows_f[pl.ds(f * CPF, CPF), CHUNK:2 * CHUNK, :] = jnp.zeros((CPF, CHUNK, 128), jnp.float32)
+        rows_c[pl.ds(f * CPF, CPF)] = value.reshape(CPF, CHUNK, 128)
+        rows_s[pl.ds(f * CPF, CPF)] = jnp.zeros((CPF, CHUNK, 128), jnp.float32)
         return 0
 
     lax.fori_loop(0, NF, one_spread, 0, unroll=4)
-    rows_f[DUMMY] = jnp.zeros((2 * CHUNK, 128), jnp.float32)
+    rows_c[DUMMY] = jnp.zeros((CHUNK, 128), jnp.float32)
+    rows_s[DUMMY] = jnp.zeros((CHUNK, 128), jnp.float32)
 
     for j, blk in enumerate(g_blocks):
         x, y, z, w, c = (blk[pl.ds(16 * k, 16), :] for k in range(5))
@@ -105,11 +105,11 @@
 
         def one_column(lg, _, j=j, blk=blk):
             start = pl.multiple_of((j * 16 + lg) * 16, 16)
-            base = pl.multiple_of((j * 16 + lg) * COL, COL)
-            cols_f[pl.ds(base, 16), :] = jnp.zeros((16, 128), jnp.float32)
+            load = pl.multiple_of((j * 16 + lg) * 8, 8)
+            cols_s[pl.ds(start, 16), :] = jnp.zeros((16, 128), jnp.float32)
             coef = blk[pl.ds(64 + lg, 1), :]
             for h in range(2):
-                cols_f[pl.ds(base + 16 + h, 1), :] = coef[:, 128 * h:128 * h + 128]
+                cols_c[pl.ds(load + h, 1), :] = coef[:, 128 * h:128 * h + 128]
             rhs[pl.ds(start, 16), :] = jnp.concatenate([take_rows(h, lg, 16) for h in range(2)], axis=1).astype(jnp.bfloat16)
             return 0
 
@@ -161,59 +161,69 @@
     per_tile = jnp.where(is_wide > 0.0, float(WIDE), float(NARROW))
     contract = (((1,), (1,)), ((), ()))
 
-    def step(code, kind):
-        take = NARROW if kind == "narrow" else WIDE
+    blank = jnp.zeros((128 - DEPTH, 128), jnp.bfloat16)
+    none = jnp.zeros((128, 128), jnp.bfloat16)
+
+    def chunks_of(code, take):
         g, q = code & 127, code >> 7
         at = [table[q + u // WIDE, u % WIDE, g] for u in range(take)]
-        times = (at[0] >> 10).astype(jnp.float32)
-        at = [e & 1023 if u % WIDE == 0 else e for u, e in enumerate(at)]
-        base = pl.multiple_of(g * COL, COL)
+        times = at[0] >> 10
+        return g, times, [e & 1023 if u % WIDE == 0 else e for u, e in enumerate(at)]
+
+    def fetch(code, kind, dist, held, u):
+        g, times, at = chunks_of(code, NARROW if kind == "narrow" else WIDE)
+        for k, value in enumerate([g, times] + at):
+            held[u, k] = value
         block = rhs[pl.ds(pl.multiple_of(g * 16, 16), 16), :]
-        blank = jnp.zeros((128 - DEPTH, AUX), jnp.bfloat16)
+        left = jnp.concatenate([lhs[e] for e in at[:4]], axis=0)
         if kind == "narrow":
-            left = jnp.concatenate(
-                [jnp.concatenate([lhs[e] for e in at[:4]], axis=0), jnp.concatenate([lhs[e] for e in at[4:]], axis=0)], axis=1)
+            left = jnp.concatenate([left, jnp.concatenate([lhs[e] for e in at[4:]], axis=0)], axis=1)
             thin = block[:, :128]
-            none = jnp.zeros((128, 128), jnp.bfloat16)
-            right = jnp.concatenate([thin, thin, thin, blank[:, :128]], axis=0)
+            right = jnp.concatenate([thin, thin, thin, blank], axis=0)
             right = jnp.concatenate([jnp.concatenate([right, none], axis=1), jnp.concatenate([none, right], axis=1)], axis=0)
-            kern = lax.rsqrt(jnp.dot(left, right, preferred_element_type=jnp.float32))
-            ka, kb = kern[:, :128], kern[:, 128:]
-            coef_a = jnp.concatenate([rows_f[e, 0:CHUNK, :] for e in at[:4]], axis=0)
-            coef_b = jnp.concatenate([rows_f[e, 0:CHUNK, :] for e in at[4:]], axis=0)
-            sec = jnp.sum((ka * coef_a + kb * coef_b).reshape(-1, 8, 128), axis=0)
-            cols_f[pl.ds(base, 8), :] = cols_f[pl.ds(base, 8), :] + sec * times
-            weight = cols_f[pl.ds(base + 16, 1), :] * times
-            sums = [rows_f[e, CHUNK:2 * CHUNK, :] for e in at]
-            first = [k[u * CHUNK:(u + 1) * CHUNK] * weight for k in (ka, kb) for u in range(4)]
         else:
-            left = jnp.concatenate([lhs[e] for e in at], axis=0)
-            if kind == "exact":
-                part = block.astype(jnp.float32)
-                dist = None
-                for k in range(3):
-                    mine = jnp.where(((pick % 16 == k) & (pick < DEPTH)), -0.5, 0.0).astype(jnp.bfloat16)
-                    mine = jnp.dot(left, mine, preferred_element_type=jnp.float32)
-                    other = part[k:k + 1] + part[8 + k:9 + k] + part[12 + k:13 + k]
-                    gap = jnp.concatenate([mine, mine], axis=1) - other
-                    dist = gap * gap if dist is None else dist + gap * gap
-                wide = spread(left, 21, 23, 1.0)
-                dist = dist + jnp.concatenate([wide, wide], axis=1) + width_row(g)
-            else:
-                right = jnp.concatenate([block, block, block, blank], axis=0)
-                dist = jnp.dot(left, right, preferred_element_type=jnp.float32)
-            kern = lax.rsqrt(dist)
-            k0, k1 = kern[:, :128], kern[:, 128:]
-            coef = jnp.concatenate([rows_f[e, 0:CHUNK, :] for e in at], axis=0)
-            sec0 = jnp.sum((k0 * coef).reshape(-1, 8, 128), axis=0)
-            sec1 = jnp.sum((k1 * coef).reshape(-1, 8, 128), axis=0)
-            cols_f[pl.ds(base, 8), :] = cols_f[pl.ds(base, 8), :] + sec0 * times
-            cols_f[pl.ds(base + 8, 8), :] = cols_f[pl.ds(base + 8, 8), :] + sec1 * times
-            both = k0 * (cols_f[pl.ds(base + 16, 1), :] * times) + k1 * (cols_f[pl.ds(base + 17, 1), :] * times)
-            sums = [rows_f[e, CHUNK:2 * CHUNK, :] for e in at]
-            first = [both[u * CHUNK:(u + 1) * CHUNK] for u in range(take)]
+            right = jnp.concatenate([block, block, block, jnp.concatenate([blank, blank], axis=1)], axis=0)
+        dist[u] = jnp.dot(left, right, preferred_element_type=jnp.float32)
+
+    def gather(at):
+        return jnp.concatenate([rows_c[e] for e in at], axis=0)
+
+    def fold(value):
+        return jnp.sum(value.reshape(-1, 8, 128), axis=0)
+
+    def apply(kern, kind, g, times, at):
+        times = times.astype(jnp.float32)
+        base = pl.multiple_of(g * 16, 16)
+        load = pl.multiple_of(g * 8, 8)
+        k0, k1 = kern[:, :128], kern[:, 128:]
+        weight = cols_c[pl.ds(load, 1), :] * times
+        if kind == "narrow":
+            second = fold(k0 * gather(at[:4]) + k1 * gather(at[4:]))
+            cols_s[pl.ds(base, 8), :] = cols_s[pl.ds(base, 8), :] + second * times
+            first = [k[u * CHUNK:(u + 1) * CHUNK] * weight for k in (k0, k1) for u in range(4)]
+        else:
+            coef = gather(at)
+            cols_s[pl.ds(base, 8), :] = cols_s[pl.ds(base, 8), :] + fold(k0 * coef) * times
+            cols_s[pl.ds(base + 8, 8), :] = cols_s[pl.ds(base + 8, 8), :] + fold(k1 * coef) * times
+            both = k0 * weight + k1 * (cols_c[pl.ds(load + 1, 1), :] * times)
+            first = [both[u * CHUNK:(u + 1) * CHUNK] for u in range(4)]
+        sums = [rows_s[e] for e in at]
         for e, value, more in zip(at, sums, first):
-            rows_f[e, CHUNK:2 * CHUNK, :] = value + more
+            rows_s[e] = value + more
+
+    def exact(code):
+        g, times, at = chunks_of(code, WIDE)
+        left = jnp.concatenate([lhs[e] for e in at], axis=0)
+        part = rhs[pl.ds(pl.multiple_of(g * 16, 16), 16), :].astype(jnp.float32)
+        wide = spread(left, 21, 23, 1.0)
+        dist = jnp.concatenate([wide, wide], axis=1) + width_row(g)
+        for k in range(3):
+            mine = jnp.where(((pick % 16 == k) & (pick < DEPTH)), -0.5, 0.0).astype(jnp.bfloat16)
+            mine = jnp.dot(left, mine, preferred_element_type=jnp.float32)
+            other = part[k:k + 1] + part[8 + k:9 + k] + part[12 + k:13 + k]
+            gap = jnp.concatenate([mine, mine], axis=1) - other
+            dist = dist + gap * gap
+        apply(lax.rsqrt(dist), "wide", g, times, at)
 
     def width_row(g):
         row = jnp.zeros((1, AUX), jnp.float32)
@@ -292,28 +302,43 @@
             copy.wait()
         count_wide, count_thin = tile_list[24, 0], tile_list[25, 0]
 
-        def many_tiles(kind, first_row, count):
+        def many_tiles(kind, first_row, last, count):
+            take = NARROW if kind == "narrow" else WIDE
+
+            def fetch_batch(b, dist, held):
+                b = jnp.minimum(b, last)
+                row, col = first_row + (b >> 4), (b & 15) * BATCH
+                for u in range(BATCH):
+                    fetch(tile_list[row, col + u], kind, dist, held, u)
+
+            def apply_batch(dist, held):
+                for u in range(BATCH):
+                    at = [held[u, 2 + k] for k in range(take)]
+                    apply(lax.rsqrt(dist[u]), kind, held[u, 0], held[u, 1], at)
+
             def body(i, _):
-                row, col = first_row + (i >> 3), (i & 7) * UNROLL
-                for u in range(UNROLL):
-                    step(tile_list[row, col + u], kind)
+                fetch_batch(2 * i + 1, dist_b, held_b)
+                apply_batch(dist_a, held_a)
+                fetch_batch(2 * i + 2, dist_a, held_a)
+                apply_batch(dist_b, held_b)
                 return 0
 
-            lax.fori_loop(0, (count + (UNROLL - 1)) // UNROLL, body, 0)
+            fetch_batch(jnp.int32(0), dist_a, held_a)
+            lax.fori_loop(0, (count + (2 * BATCH - 1)) // (2 * BATCH), body, 0)
 
         @pl.when(safe)
         def _():
-            many_tiles("wide", 0, count_wide)
-            many_tiles("narrow", 16, count_thin)
+            many_tiles("wide", 0, 255, count_wide)
+            many_tiles("narrow", 16, 127, count_thin)
 
         @pl.when(jnp.logical_not(safe))
         def _():
             def wide_one(t, _):
-                step(tile_list[t >> 7, t & 127], "exact")
+                exact(tile_list[t >> 7, t & 127])
                 return 0
 
             def thin_one(t, _):
-                step(tile_list[16 + (t >> 8), (t & 255) >> 1] + 128 * (t & 1), "exact")
+                exact(tile_list[16 + (t >> 8), (t & 255) >> 1] + 128 * (t & 1))
                 return 0
 
             lax.fori_loop(0, count_wide, wide_one, 0)
@@ -328,19 +353,19 @@
     lanes = lax.broadcasted_iota(jnp.int32, (AUX, 128), 1)
 
     def collect(f, out):
-        col = jnp.sum(rows_f[pl.ds(f * CPF, CPF), CHUNK:2 * CHUNK, :].reshape(AUX, 128), axis=1, keepdims=True)
+        col = jnp.sum(rows_s[pl.ds(f * CPF, CPF)].reshape(AUX, 128), axis=1, keepdims=True)
         return jnp.where(lanes == f, col, out)
 
-    rows_out = rows_f[pl.ds(0, CPF), 0:CHUNK, :].reshape(AUX, 128)
+    rows_out = rows_c[pl.ds(0, CPF)].reshape(AUX, 128)
     rows_out = lax.fori_loop(0, NF, collect, rows_out).T
     outf_own[...] = rows_out[0:16]
     outf_near[...] = rows_out[16:32]
     outf_far[...] = rows_out[32:64]
     cols = []
     for h in range(2):
-        half = cols_f[pl.ds(8 * h, NG, stride=COL), :]
+        half = cols_s[pl.ds(8 * h, NG, stride=16), :]
         for r in range(1, 8):
-            half = half + cols_f[pl.ds(8 * h + r, NG, stride=COL), :]
+            half = half + cols_s[pl.ds(8 * h + r, NG, stride=16), :]
         cols.append(half)
     cols = jnp.concatenate(cols, axis=1)
     out_own[...] = cols[0:16]
@@ -359,8 +384,10 @@
         out_specs=(vmem,) * 7,
         scratch_shapes=[
             pltpu.VMEM((DUMMY + 1, CHUNK, 128), jnp.bfloat16),
-            pltpu.VMEM((DUMMY + 1, 2 * CHUNK, 128), jnp.float32),
-            pltpu.VMEM((NG * COL, 128), jnp.float32),
+            pltpu.VMEM((DUMMY + 1, CHUNK, 128), jnp.float32),
+            pltpu.VMEM((DUMMY + 1, CHUNK, 128), jnp.float32),
+            pltpu.VMEM((NG * 16, 128), jnp.float32),
+            pltpu.VMEM((NG * 8, 128), jnp.float32),
             pltpu.VMEM((NG * 16, AUX), jnp.bfloat16),
             pltpu.VMEM((2, DEPTH * 16, 128), jnp.float32),
             pltpu.VMEM((8, AUX), jnp.float32),
@@ -371,8 +398,12 @@
             pltpu.VMEM((2, 128, 128), jnp.float32),
             pltpu.VMEM((SPAN // WIDE + 2, WIDE, 128), jnp.int32),
             pltpu.VMEM((32, 128), jnp.int32),
+            pltpu.VMEM((BATCH, 128, AUX), jnp.float32),
+            pltpu.VMEM((BATCH, 128, AUX), jnp.float32),
             pltpu.SMEM((SPAN // WIDE + 2, WIDE, 128), jnp.int32),
             pltpu.SMEM((32, 128), jnp.int32),
+            pltpu.SMEM((BATCH, 16), jnp.int32),
+            pltpu.SMEM((BATCH, 16), jnp.int32),
             pltpu.SemaphoreType.DMA((2,)),
         ],
         compiler_params=pltpu.CompilerParams(vmem_limit_bytes=56 * 2**20),

time: 254 us -> 250 us (0.984)
  the two profiles are of different devices: /device:TPU:0 before, /device:TPU:8 now
where the time goes in v1:
time: 250 us; the launch traced here: 251 us
  Pallas kernels  191 us (76%)
  starting transfers between devices  35.6 us (14%)
  waiting for transfers between devices  17.4 us (7%)
  other arithmetic  3.81 us (2%)
  local copies, waits for them, and re-layouts  2.52 us (1%)
    pallas_call x1, Pallas kernels, rectangle(): pl.pallas_call(pair_kernel, out_shape=(shape(64), shape(32), shape(16), s...  191 us
    ppermute x15, starting transfers between devices, swap(): return lax.ppermute(array, 'frag', pairs)  35.6 us
    ppermute x15, waiting for transfers between devices, swap(): return lax.ppermute(array, 'frag', pairs)  17.4 us
  transfers between devices with their start and end apart: 15, of which 8 were waited for; matrix products, arithmetic and copies ran while one was open for 1% of the time, Pallas kernels for 0%

profile of v1, /device:TPU:8, one launch (start us, length us, event | category | flops | bytes accessed | tf_op | source)
XLA Modules:
  0.0 250.9 jit_solution(17006759360473485465)
XLA Ops:
  0.0 0.7 convert_bitcast_fusion.1
  0.7 0.7 convert_bitcast_fusion
  1.4 0.8 fusion.4
  2.2 1.6 collective-permute-start.3
  3.8 2.1 collective-permute-start.4
  5.9 4.0 %collective-permute-start.1 = (f32[96,256]{1,0:T(8,128)S(1)}, f32[96,256]{1,0:T(8,128)S(1)}, u32[]{:S(2)}, u32[]{:S(2)}) collective-permute-start(f32[96,256]{1,0:T(8,128)S(1)} %select_maximum_fusion.refs_0_), channel_id=1, source_target_pairs={{0,24},{1,25},{2,26},{3,27},{4,28},{5,29},{6,30},{7,31},{8,16},{9,... | collective-permute-start | bytes 294920 | tf_op jit(solution)/shard_map/ppermute | solution.py:432
  10.0 1.2 collective-permute-start.5
  11.4 0.5 collective-permute-start.8
  11.9 2.7 %collective-permute-done.refs_1_ = f32[96,256]{1,0:T(8,128)S(1)} collective-permute-done((f32[96,256]{1,0:T(8,128)S(1)}, f32[96,256]{1,0:T(8,128)S(1)}, u32[]{:S(2)}, u32[]{:S(2)}) %collective-permute-start) | collective-permute-done | bytes 98336 | tf_op jit(solution)/shard_map/ppermute | solution.py:432
  14.9 1.0 collective-permute-done.5.refs_6_
  16.0 0.6 concatenate.7.meta
  16.6 3.8 %collective-permute-done.2.refs_3_ = f32[96,256]{1,0:T(8,128)S(1)} collective-permute-done((f32[96,256]{1,0:T(8,128)S(1)}, f32[96,256]{1,0:T(8,128)S(1)}, u32[]{:S(2)}, u32[]{:S(2)}) %collective-permute-start.2) | collective-permute-done | bytes 98336 | tf_op jit(solution)/shard_map/ppermute | solution.py:432
  20.5 0.5 copy-done.9
  21.1 0.6 copy-done.10
  21.7 191.3 %shard_map.46 = (f32[64,256]{1,0:T(8,128)}, f32[32,256]{1,0:T(8,128)}, f32[16,256]{1,0:T(8,128)}, f32[16,256]{1,0:T(8,128)}, f32[32,256]{1,0:T(8,128)}, /*index=5*/f32[16,256]{1,0:T(8,128)}, f32[16,256]{1,0:T(8,128)}) custom-call(s32[20]{0:T(128)} %concatenate.7.meta, f32[96,256]{1,0:T(8,128)} %copy-done, f32[96,256]{1,0:T(8,128)} %copy-done.5, ...), custom_call_target="tpu_custom_call" | custom-call | tf_op jit(solution)/shard_map/pallas_call | solution.py:380
  213.0 25.7 %collective-permute-start.12 = (f32[64,256]{1,0:T(8,128)}, f32[64,256]{1,0:T(8,128)S(1)}, u32[]{:S(2)}, u32[]{:S(2)}) collective-permute-start(f32[64,256]{1,0:T(8,128)} %get-tuple-element.16), channel_id=1, source_target_pairs={{0,1},{1,0},{2,3},{3,2},{4,5},{5,4},{6,7},{7,6},{8,9},{9,8},{10,11... | collective-permute-start | bytes 196616 | tf_op jit(solution)/shard_map/ppermute | solution.py:432
  238.7 1.1 collective-permute-done.12
  239.8 0.8 slice_add_fusion
  240.6 3.4 %collective-permute-done.10 = f32[32,256]{1,0:T(8,128)S(1)} collective-permute-done((f32[32,256]{1,0:T(8,128)}, f32[32,256]{1,0:T(8,128)S(1)}, u32[]{:S(2)}, u32[]{:S(2)}) %collective-permute-start.10) | collective-permute-done | bytes 32800 | tf_op jit(solution)/shard_map/ppermute | solution.py:432
  244.1 1.6 collective-permute-done.13
  245.8 2.0 collective-permute-done.11
  247.8 1.7 collective-permute-done.14
  249.5 0.6 copy-done.16
  250.2 0.7 fusion.1
  (55 shorter events, 0.8 us)
Async XLA Ops:
  2.2 18.2 %copy-start = (f32[96,256]{1,0:T(8,128)}, f32[96,256]{1,0:T(8,128)S(1)}, u32[]{:S(2)}) copy-start(f32[96,256]{1,0:T(8,128)S(1)} %select_maximum_fusion.refs_0_) | copy-start | bytes 294916
  2.2 7.7 %collective-permute-start.3 = (f32[96,256]{1,0:T(8,128)S(1)}, f32[96,256]{1,0:T(8,128)S(1)}, u32[]{:S(2)}, u32[]{:S(2)}) collective-permute-start(f32[96,256]{1,0:T(8,128)S(1)} %select_maximum_fusion.refs_0_), channel_id=1, source_target_pairs={{0,2},{1,3},{2,0},{3,1},{4,6},{5,7},{6,4},{7,5},{8,10},{9,11},{10,... | collective-permute-start | bytes 294920 | tf_op jit(solution)/shard_map/ppermute | solution.py:432
  3.8 7.5 %collective-permute-start.6 = (f32[96,256]{1,0:T(8,128)S(1)}, f32[96,256]{1,0:T(8,128)S(1)}, u32[]{:S(2)}, u32[]{:S(2)}) collective-permute-start(f32[96,256]{1,0:T(8,128)S(1)} %select_maximum_fusion.refs_0_), channel_id=1, source_target_pairs={{0,1},{1,0},{2,3},{3,2},{4,5},{5,4},{6,7},{7,6},{8,9},{9,8},{10,11... | collective-permute-start | bytes 294920 | tf_op jit(solution)/shard_map/ppermute | solution.py:432
  3.8 7.5 %collective-permute-start.4 = (f32[96,256]{1,0:T(8,128)S(1)}, f32[96,256]{1,0:T(8,128)S(1)}, u32[]{:S(2)}, u32[]{:S(2)}) collective-permute-start(f32[96,256]{1,0:T(8,128)S(1)} %select_maximum_fusion.refs_0_), channel_id=1, source_target_pairs={{0,6},{1,7},{2,4},{3,5},{4,2},{5,3},{6,0},{7,1},{8,14},{9,15},{10,... | collective-permute-start | bytes 294920 | tf_op jit(solution)/shard_map/ppermute | solution.py:432
  5.9 10.7 %collective-permute-start.1 = (f32[96,256]{1,0:T(8,128)S(1)}, f32[96,256]{1,0:T(8,128)S(1)}, u32[]{:S(2)}, u32[]{:S(2)}) collective-permute-start(f32[96,256]{1,0:T(8,128)S(1)} %select_maximum_fusion.refs_0_), channel_id=1, source_target_pairs={{0,24},{1,25},{2,26},{3,27},{4,28},{5,29},{6,30},{7,31},{8,16},{9,... | collective-permute-start | bytes 294920 | tf_op jit(solution)/shard_map/ppermute | solution.py:432
  10.0 4.6 %collective-permute-start = (f32[96,256]{1,0:T(8,128)S(1)}, f32[96,256]{1,0:T(8,128)S(1)}, u32[]{:S(2)}, u32[]{:S(2)}) collective-permute-start(f32[96,256]{1,0:T(8,128)S(1)} %select_maximum_fusion.refs_0_), channel_id=1, source_target_pairs={{0,8},{1,9},{2,10},{3,11},{4,12},{5,13},{6,14},{7,15},{8,0},{9,1},... | collective-permute-start | bytes 294920 | tf_op jit(solution)/shard_map/ppermute | solution.py:432
  10.0 10.5 %copy-start.1 = (f32[96,256]{1,0:T(8,128)}, f32[96,256]{1,0:T(8,128)S(1)}, u32[]{:S(2)}) copy-start(f32[96,256]{1,0:T(8,128)S(1)} %collective-permute-done.3.refs_4_) | copy-start | bytes 294916
  10.0 5.9 %collective-permute-start.5 = (f32[96,256]{1,0:T(8,128)S(1)}, f32[96,256]{1,0:T(8,128)S(1)}, u32[]{:S(2)}, u32[]{:S(2)}) collective-permute-start(f32[96,256]{1,0:T(8,128)S(1)} %collective-permute-done.3.refs_4_), channel_id=1, source_target_pairs={{0,6},{1,7},{2,4},{3,5},{4,2},{5,3},{6,0},{7,1},{8,14},{9,15},{10,... | collective-permute-start | bytes 294920 | tf_op jit(solution)/shard_map/ppermute | solution.py:432
  11.3 9.2 %copy-start.2 = (f32[96,256]{1,0:T(8,128)}, f32[96,256]{1,0:T(8,128)S(1)}, u32[]{:S(2)}) copy-start(f32[96,256]{1,0:T(8,128)S(1)} %collective-permute-done.6.refs_7_) | copy-start | bytes 294916
  11.3 5.4 %collective-permute-start.7 = (f32[96,256]{1,0:T(8,128)S(1)}, f32[96,256]{1,0:T(8,128)S(1)}, u32[]{:S(2)}, u32[]{:S(2)}) collective-permute-start(f32[96,256]{1,0:T(8,128)S(1)} %collective-permute-done.3.refs_4_), channel_id=1, source_target_pairs={{0,1},{1,0},{2,3},{3,2},{4,5},{5,4},{6,7},{7,6},{8,9},{9,8},{10,11... | collective-permute-start | bytes 294920 | tf_op jit(solution)/shard_map/ppermute | solution.py:432
  11.4 9.1 %copy-start.3 = (f32[96,256]{1,0:T(8,128)}, f32[96,256]{1,0:T(8,128)S(1)}, u32[]{:S(2)}) copy-start(f32[96,256]{1,0:T(8,128)S(1)} %collective-permute-done.4.refs_5_) | copy-start | bytes 294916
  11.4 5.2 %collective-permute-start.8 = (f32[96,256]{1,0:T(8,128)S(1)}, f32[96,256]{1,0:T(8,128)S(1)}, u32[]{:S(2)}, u32[]{:S(2)}) collective-permute-start(f32[96,256]{1,0:T(8,128)S(1)} %collective-permute-done.4.refs_5_), channel_id=1, source_target_pairs={{0,1},{1,0},{2,3},{3,2},{4,5},{5,4},{6,7},{7,6},{8,9},{9,8},{10,11... | collective-permute-start | bytes 294920 | tf_op jit(solution)/shard_map/ppermute | solution.py:432
  14.6 5.9 %copy-start.5 = (f32[96,256]{1,0:T(8,128)}, f32[96,256]{1,0:T(8,128)S(1)}, u32[]{:S(2)}) copy-start(f32[96,256]{1,0:T(8,128)S(1)} %collective-permute-done.refs_1_) | copy-start | bytes 294916
  14.6 5.8 %collective-permute-start.2 = (f32[96,256]{1,0:T(8,128)S(1)}, f32[96,256]{1,0:T(8,128)S(1)}, u32[]{:S(2)}, u32[]{:S(2)}) collective-permute-start(f32[96,256]{1,0:T(8,128)S(1)} %collective-permute-done.refs_1_), channel_id=1, source_target_pairs={{0,24},{1,25},{2,26},{3,27},{4,28},{5,29},{6,30},{7,31},{8,16},{9,... | collective-permute-start | bytes 294920 | tf_op jit(solution)/shard_map/ppermute | solution.py:432
  15.9 4.6 %copy-start.6 = (f32[96,256]{1,0:T(8,128)}, f32[96,256]{1,0:T(8,128)S(1)}, u32[]{:S(2)}) copy-start(f32[96,256]{1,0:T(8,128)S(1)} %collective-permute-done.5.refs_6_) | copy-start | bytes 294916
  15.9 4.5 %collective-permute-start.9 = (f32[96,256]{1,0:T(8,128)S(1)}, f32[96,256]{1,0:T(8,128)S(1)}, u32[]{:S(2)}, u32[]{:S(2)}) collective-permute-start(f32[96,256]{1,0:T(8,128)S(1)} %collective-permute-done.5.refs_6_), channel_id=1, source_target_pairs={{0,1},{1,0},{2,3},{3,2},{4,5},{5,4},{6,7},{7,6},{8,9},{9,8},{10,11... | collective-permute-start | bytes 294920 | tf_op jit(solution)/shard_map/ppermute | solution.py:432
  16.6 3.9 %copy-start.4 = (f32[96,256]{1,0:T(8,128)}, f32[96,256]{1,0:T(8,128)S(1)}, u32[]{:S(2)}) copy-start(f32[96,256]{1,0:T(8,128)S(1)} %collective-permute-done.1.refs_2_) | copy-start | bytes 294916
  16.6 3.9 %copy-start.8 = (f32[96,256]{1,0:T(8,128)}, f32[96,256]{1,0:T(8,128)S(1)}, u32[]{:S(2)}) copy-start(f32[96,256]{1,0:T(8,128)S(1)} %collective-permute-done.8.refs_9_) | copy-start | bytes 294916
  213.0 26.8 %collective-permute-start.12 = (f32[64,256]{1,0:T(8,128)}, f32[64,256]{1,0:T(8,128)S(1)}, u32[]{:S(2)}, u32[]{:S(2)}) collective-permute-start(f32[64,256]{1,0:T(8,128)} %get-tuple-element.16), channel_id=1, source_target_pairs={{0,1},{1,0},{2,3},{3,2},{4,5},{5,4},{6,7},{7,6},{8,9},{9,8},{10,11... | collective-permute-start | bytes 196616 | tf_op jit(solution)/shard_map/ppermute | solution.py:432
  238.7 5.3 %collective-permute-start.10 = (f32[32,256]{1,0:T(8,128)}, f32[32,256]{1,0:T(8,128)S(1)}, u32[]{:S(2)}, u32[]{:S(2)}) collective-permute-start(f32[32,256]{1,0:T(8,128)} %get-tuple-element.13), channel_id=1, source_target_pairs={{0,24},{1,25},{2,26},{3,27},{4,28},{5,29},{6,30},{7,31},{8,16},{9,... | collective-permute-start | bytes 98312 | tf_op jit(solution)/shard_map/ppermute | solution.py:432
  239.8 4.2 %copy-start.12 = (f32[16,256]{1,0:T(8,128)S(1)}, f32[16,256]{1,0:T(8,128)}, u32[]{:S(2)}) copy-start(f32[16,256]{1,0:T(8,128)} %get-tuple-element.14) | copy-start | bytes 49156
  240.6 5.1 %collective-permute-start.13 = (f32[32,256]{1,0:T(8,128)S(1)}, f32[32,256]{1,0:T(8,128)S(1)}, u32[]{:S(2)}, u32[]{:S(2)}) collective-permute-start(f32[32,256]{1,0:T(8,128)S(1)} %slice_add_fusion), channel_id=1, source_target_pairs={{0,6},{1,7},{2,4},{3,5},{4,2},{5,3},{6,0},{7,1},{8,14},{9,15},{10,... | collective-permute-start | bytes 98312 | tf_op jit(solution)/shard_map/ppermute | solution.py:432
  244.0 3.8 %collective-permute-start.11 = (f32[16,256]{1,0:T(8,128)S(1)}, f32[16,256]{1,0:T(8,128)S(1)}, u32[]{:S(2)}, u32[]{:S(2)}) collective-permute-start(f32[16,256]{1,0:T(8,128)S(1)} %slice_add_fusion.5), channel_id=1, source_target_pairs={{0,8},{1,9},{2,10},{3,11},{4,12},{5,13},{6,14},{7,15},{8,0},{9,1},... | collective-permute-start | bytes 49160 | tf_op jit(solution)/shard_map/ppermute | solution.py:432
  245.7 3.8 %collective-permute-start.14 = (f32[16,256]{1,0:T(8,128)S(1)}, f32[16,256]{1,0:T(8,128)S(1)}, u32[]{:S(2)}, u32[]{:S(2)}) collective-permute-start(f32[16,256]{1,0:T(8,128)S(1)} %slice_add_fusion.1), channel_id=1, source_target_pairs={{0,2},{1,3},{2,0},{3,1},{4,6},{5,7},{6,4},{7,5},{8,10},{9,11},{10,... | collective-permute-start | bytes 49160 | tf_op jit(solution)/shard_map/ppermute | solution.py:432
  (8 other events, 17.4 us)

commit v2 on v1

--- a/solution.py
+++ b/solution.py
@@ -19,7 +19,8 @@
 SPAN = 64
 DUMMY = NF * CPF
 DEPTH = 48
-BATCH = 8
+BATCH = 16
+SHIFT = 3
 WIDTH_FLOOR = 1.0 / 32.0
 
 
@@ -34,7 +35,7 @@
     packets = refs[:11]
     out_sib, out_far, out_near, out_own, outf_far, outf_near, outf_own = refs[11:18]
     (lhs, rows_c, rows_s, cols_s, cols_c, rhs, build, slots, counts, chunks, zeros_v, places, ends,
-     table_v, tiles_v, dist_a, dist_b, table, tile_list, held_a, held_b, sem) = refs[18:]
+     table_v, tiles_v, row_sums, table, tile_list, sem) = refs[18:]
     f_blocks = [packets[0], packets[1], packets[2], packets[3]]
     g_blocks = [packets[0]] + list(packets[4:])
     plane = meta[0]
@@ -166,14 +167,12 @@
 
     def chunks_of(code, take):
         g, q = code & 127, code >> 7
-        at = [table[q + u // WIDE, u % WIDE, g] for u in range(take)]
+        views = [table.at[q + v, :, pl.ds(g, 1)] for v in range(take // WIDE)]
+        at = [views[u // WIDE][u % WIDE, 0] for u in range(take)]
         times = at[0] >> 10
         return g, times, [e & 1023 if u % WIDE == 0 else e for u, e in enumerate(at)]
 
-    def fetch(code, kind, dist, held, u):
-        g, times, at = chunks_of(code, NARROW if kind == "narrow" else WIDE)
-        for k, value in enumerate([g, times] + at):
-            held[u, k] = value
+    def distances(g, at, kind):
         block = rhs[pl.ds(pl.multiple_of(g * 16, 16), 16), :]
         left = jnp.concatenate([lhs[e] for e in at[:4]], axis=0)
         if kind == "narrow":
@@ -183,7 +182,7 @@
             right = jnp.concatenate([jnp.concatenate([right, none], axis=1), jnp.concatenate([none, right], axis=1)], axis=0)
         else:
             right = jnp.concatenate([block, block, block, jnp.concatenate([blank, blank], axis=1)], axis=0)
-        dist[u] = jnp.dot(left, right, preferred_element_type=jnp.float32)
+        return jnp.dot(left, right, preferred_element_type=jnp.float32)
 
     def gather(at):
         return jnp.concatenate([rows_c[e] for e in at], axis=0)
@@ -302,34 +301,22 @@
             copy.wait()
         count_wide, count_thin = tile_list[24, 0], tile_list[25, 0]
 
-        def many_tiles(kind, first_row, last, count):
+        def many_tiles(kind, first_row, count):
             take = NARROW if kind == "narrow" else WIDE
 
-            def fetch_batch(b, dist, held):
-                b = jnp.minimum(b, last)
-                row, col = first_row + (b >> 4), (b & 15) * BATCH
+            def body(b, _):
+                row, col = first_row + lax.shift_right_logical(b, SHIFT), (b & (128 // BATCH - 1)) * BATCH
                 for u in range(BATCH):
-                    fetch(tile_list[row, col + u], kind, dist, held, u)
-
-            def apply_batch(dist, held):
-                for u in range(BATCH):
-                    at = [held[u, 2 + k] for k in range(take)]
-                    apply(lax.rsqrt(dist[u]), kind, held[u, 0], held[u, 1], at)
-
-            def body(i, _):
-                fetch_batch(2 * i + 1, dist_b, held_b)
-                apply_batch(dist_a, held_a)
-                fetch_batch(2 * i + 2, dist_a, held_a)
-                apply_batch(dist_b, held_b)
+                    g, times, at = chunks_of(tile_list[row, col + u], take)
+                    apply(lax.rsqrt(distances(g, at, kind)), kind, g, times, at)
                 return 0
 
-            fetch_batch(jnp.int32(0), dist_a, held_a)
-            lax.fori_loop(0, (count + (2 * BATCH - 1)) // (2 * BATCH), body, 0)
+            lax.fori_loop(0, (count + (BATCH - 1)) // BATCH, body, 0)
 
         @pl.when(safe)
         def _():
-            many_tiles("wide", 0, 255, count_wide)
-            many_tiles("narrow", 16, 127, count_thin)
+            many_tiles("wide", 0, count_wide)
+            many_tiles("narrow", 16, count_thin)
 
         @pl.when(jnp.logical_not(safe))
         def _():
@@ -350,14 +337,19 @@
     upto = (lax.broadcasted_iota(jnp.int32, (128, 128), 1) <= pick).astype(jnp.float32).astype(jnp.bfloat16)
     lax.while_loop(lambda state: state[0] * SPAN < state[1], one_round, (jnp.int32(0), jnp.int32(1)))
 
-    lanes = lax.broadcasted_iota(jnp.int32, (AUX, 128), 1)
-
-    def collect(f, out):
-        col = jnp.sum(rows_s[pl.ds(f * CPF, CPF)].reshape(AUX, 128), axis=1, keepdims=True)
-        return jnp.where(lanes == f, col, out)
-
-    rows_out = rows_c[pl.ds(0, CPF)].reshape(AUX, 128)
-    rows_out = lax.fori_loop(0, NF, collect, rows_out).T
+    ones8 = jnp.ones((8, 256), jnp.bfloat16)
+
+    def collect(f, _):
+        value = rows_s[pl.ds(f * CPF, CPF)].reshape(AUX, 128)
+        high = value.astype(jnp.bfloat16)
+        low = (value - high.astype(jnp.float32)).astype(jnp.bfloat16)
+        row = lax.dot_general(ones8, jnp.concatenate([high, low], axis=1), contract, preferred_element_type=jnp.float32)
+        for h in range(2):
+            row_sums[h, pl.ds(f, 1), :] = row[0:1, 128 * h:128 * h + 128]
+        return 0
+
+    lax.fori_loop(0, NF, collect, 0, unroll=8)
+    rows_out = jnp.concatenate([row_sums[0], row_sums[1]], axis=1)
     outf_own[...] = rows_out[0:16]
     outf_near[...] = rows_out[16:32]
     outf_far[...] = rows_out[32:64]
@@ -398,12 +390,9 @@
             pltpu.VMEM((2, 128, 128), jnp.float32),
             pltpu.VMEM((SPAN // WIDE + 2, WIDE, 128), jnp.int32),
             pltpu.VMEM((32, 128), jnp.int32),
-            pltpu.VMEM((BATCH, 128, AUX), jnp.float32),
-            pltpu.VMEM((BATCH, 128, AUX), jnp.float32),
+            pltpu.VMEM((2, NF, 128), jnp.float32),
             pltpu.SMEM((SPAN // WIDE + 2, WIDE, 128), jnp.int32),
             pltpu.SMEM((32, 128), jnp.int32),
-            pltpu.SMEM((BATCH, 16), jnp.int32),
-            pltpu.SMEM((BATCH, 16), jnp.int32),
             pltpu.SemaphoreType.DMA((2,)),
         ],
         compiler_params=pltpu.CompilerParams(vmem_limit_bytes=56 * 2**20),

time: 250 us -> 250 us (level)
  the two profiles are of different devices: /device:TPU:8 before, /device:TPU:0 now
where the time goes in v2:
time: 250 us; the launch traced here: 248 us
  Pallas kernels  190 us (76%)
  starting transfers between devices  37.4 us (15%)
  waiting for transfers between devices  13.9 us (6%)
  other arithmetic  3.81 us (2%)
  local copies, waits for them, and re-layouts  2.52 us (1%)
    pallas_call x1, Pallas kernels, rectangle(): pl.pallas_call(pair_kernel, out_shape=(shape(64), shape(32), shape(16), s...  190 us
    ppermute x15, starting transfers between devices, swap(): return lax.ppermute(array, 'frag', pairs)  37.4 us
    ppermute x15, waiting for transfers between devices, swap(): return lax.ppermute(array, 'frag', pairs)  13.9 us
  transfers between devices with their start and end apart: 15, of which 6 were waited for; matrix products, arithmetic and copies ran while one was open for 1% of the time, Pallas kernels for 0%

profile of v2, /device:TPU:0, one launch (start us, length us, event | category | flops | bytes accessed | tf_op | source)
XLA Modules:
  0.0 248.2 jit_solution(4748559026465408416)
XLA Ops:
  0.0 0.7 convert_bitcast_fusion.1
  0.7 0.7 convert_bitcast_fusion
  1.4 0.8 fusion.4
  2.2 1.7 collective-permute-start.3
  3.9 2.1 collective-permute-start.4
  6.0 4.0 %collective-permute-start.1 = (f32[96,256]{1,0:T(8,128)S(1)}, f32[96,256]{1,0:T(8,128)S(1)}, u32[]{:S(2)}, u32[]{:S(2)}) collective-permute-start(f32[96,256]{1,0:T(8,128)S(1)} %select_maximum_fusion.refs_0_), channel_id=1, source_target_pairs={{0,24},{1,25},{2,26},{3,27},{4,28},{5,29},{6,30},{7,31},{8,16},{9,... | collective-permute-start | bytes 294920 | tf_op jit(solution)/shard_map/ppermute | solution.py:421
  10.0 1.2 collective-permute-start.5
  11.5 0.5 collective-permute-start.8
  12.0 2.7 %collective-permute-done.refs_1_ = f32[96,256]{1,0:T(8,128)S(1)} collective-permute-done((f32[96,256]{1,0:T(8,128)S(1)}, f32[96,256]{1,0:T(8,128)S(1)}, u32[]{:S(2)}, u32[]{:S(2)}) %collective-permute-start) | collective-permute-done | bytes 98336 | tf_op jit(solution)/shard_map/ppermute | solution.py:421
  15.0 1.0 collective-permute-done.5.refs_6_
  16.1 0.6 concatenate.7.meta
  16.7 3.8 %collective-permute-done.2.refs_3_ = f32[96,256]{1,0:T(8,128)S(1)} collective-permute-done((f32[96,256]{1,0:T(8,128)S(1)}, f32[96,256]{1,0:T(8,128)S(1)}, u32[]{:S(2)}, u32[]{:S(2)}) %collective-permute-start.2) | collective-permute-done | bytes 98336 | tf_op jit(solution)/shard_map/ppermute | solution.py:421
  20.6 0.5 copy-done.9
  21.1 0.6 copy-done.10
  21.8 190.4 %shard_map.46 = (f32[64,256]{1,0:T(8,128)}, f32[32,256]{1,0:T(8,128)}, f32[16,256]{1,0:T(8,128)}, f32[16,256]{1,0:T(8,128)}, f32[32,256]{1,0:T(8,128)}, /*index=5*/f32[16,256]{1,0:T(8,128)}, f32[16,256]{1,0:T(8,128)}) custom-call(s32[20]{0:T(128)} %concatenate.7.meta, f32[96,256]{1,0:T(8,128)} %copy-done, f32[96,256]{1,0:T(8,128)} %copy-done.5, ...), custom_call_target="tpu_custom_call" | custom-call | tf_op jit(solution)/shard_map/pallas_call | solution.py:372
  212.2 5.8 %collective-permute-start.12 = (f32[64,256]{1,0:T(8,128)}, f32[64,256]{1,0:T(8,128)S(1)}, u32[]{:S(2)}, u32[]{:S(2)}) collective-permute-start(f32[64,256]{1,0:T(8,128)} %get-tuple-element.16), channel_id=1, source_target_pairs={{0,1},{1,0},{2,3},{3,2},{4,5},{5,4},{6,7},{7,6},{8,9},{9,8},{10,11... | collective-permute-start | bytes 196616 | tf_op jit(solution)/shard_map/ppermute | solution.py:421
  218.0 15.0 %collective-permute-start.10 = (f32[32,256]{1,0:T(8,128)}, f32[32,256]{1,0:T(8,128)S(1)}, u32[]{:S(2)}, u32[]{:S(2)}) collective-permute-start(f32[32,256]{1,0:T(8,128)} %get-tuple-element.13), channel_id=1, source_target_pairs={{0,24},{1,25},{2,26},{3,27},{4,28},{5,29},{6,30},{7,31},{8,16},{9,... | collective-permute-start | bytes 98312 | tf_op jit(solution)/shard_map/ppermute | solution.py:421
  233.0 0.8 slice_add_fusion
  234.2 1.0 collective-permute-done.10
  235.3 3.6 %collective-permute-done.13 = f32[32,256]{1,0:T(8,128)S(1)} collective-permute-done((f32[32,256]{1,0:T(8,128)S(1)}, f32[32,256]{1,0:T(8,128)S(1)}, u32[]{:S(2)}, u32[]{:S(2)}) %collective-permute-start.13) | collective-permute-done | bytes 32800 | tf_op jit(solution)/shard_map/ppermute | solution.py:421
  238.9 6.2 %collective-permute-start.14 = (f32[16,256]{1,0:T(8,128)S(1)}, f32[16,256]{1,0:T(8,128)S(1)}, u32[]{:S(2)}, u32[]{:S(2)}) collective-permute-start(f32[16,256]{1,0:T(8,128)S(1)} %slice_add_fusion.1), channel_id=1, source_target_pairs={{0,2},{1,3},{2,0},{3,1},{4,6},{5,7},{6,4},{7,5},{8,10},{9,11},{10,... | collective-permute-start | bytes 49160 | tf_op jit(solution)/shard_map/ppermute | solution.py:421
  245.2 1.7 collective-permute-done.14
  246.9 0.6 copy-done.16
  247.5 0.7 fusion.1
  (55 shorter events, 1.2 us)
Async XLA Ops:
  2.2 18.3 %copy-start = (f32[96,256]{1,0:T(8,128)}, f32[96,256]{1,0:T(8,128)S(1)}, u32[]{:S(2)}) copy-start(f32[96,256]{1,0:T(8,128)S(1)} %select_maximum_fusion.refs_0_) | copy-start | bytes 294916
  2.2 7.8 %collective-permute-start.3 = (f32[96,256]{1,0:T(8,128)S(1)}, f32[96,256]{1,0:T(8,128)S(1)}, u32[]{:S(2)}, u32[]{:S(2)}) collective-permute-start(f32[96,256]{1,0:T(8,128)S(1)} %select_maximum_fusion.refs_0_), channel_id=1, source_target_pairs={{0,2},{1,3},{2,0},{3,1},{4,6},{5,7},{6,4},{7,5},{8,10},{9,11},{10,... | collective-permute-start | bytes 294920 | tf_op jit(solution)/shard_map/ppermute | solution.py:421
  3.9 7.5 %collective-permute-start.6 = (f32[96,256]{1,0:T(8,128)S(1)}, f32[96,256]{1,0:T(8,128)S(1)}, u32[]{:S(2)}, u32[]{:S(2)}) collective-permute-start(f32[96,256]{1,0:T(8,128)S(1)} %select_maximum_fusion.refs_0_), channel_id=1, source_target_pairs={{0,1},{1,0},{2,3},{3,2},{4,5},{5,4},{6,7},{7,6},{8,9},{9,8},{10,11... | collective-permute-start | bytes 294920 | tf_op jit(solution)/shard_map/ppermute | solution.py:421
  3.9 7.5 %collective-permute-start.4 = (f32[96,256]{1,0:T(8,128)S(1)}, f32[96,256]{1,0:T(8,128)S(1)}, u32[]{:S(2)}, u32[]{:S(2)}) collective-permute-start(f32[96,256]{1,0:T(8,128)S(1)} %select_maximum_fusion.refs_0_), channel_id=1, source_target_pairs={{0,6},{1,7},{2,4},{3,5},{4,2},{5,3},{6,0},{7,1},{8,14},{9,15},{10,... | collective-permute-start | bytes 294920 | tf_op jit(solution)/shard_map/ppermute | solution.py:421
  6.0 10.7 %collective-permute-start.1 = (f32[96,256]{1,0:T(8,128)S(1)}, f32[96,256]{1,0:T(8,128)S(1)}, u32[]{:S(2)}, u32[]{:S(2)}) collective-permute-start(f32[96,256]{1,0:T(8,128)S(1)} %select_maximum_fusion.refs_0_), channel_id=1, source_target_pairs={{0,24},{1,25},{2,26},{3,27},{4,28},{5,29},{6,30},{7,31},{8,16},{9,... | collective-permute-start | bytes 294920 | tf_op jit(solution)/shard_map/ppermute | solution.py:421
  10.0 4.6 %collective-permute-start = (f32[96,256]{1,0:T(8,128)S(1)}, f32[96,256]{1,0:T(8,128)S(1)}, u32[]{:S(2)}, u32[]{:S(2)}) collective-permute-start(f32[96,256]{1,0:T(8,128)S(1)} %select_maximum_fusion.refs_0_), channel_id=1, source_target_pairs={{0,8},{1,9},{2,10},{3,11},{4,12},{5,13},{6,14},{7,15},{8,0},{9,1},... | collective-permute-start | bytes 294920 | tf_op jit(solution)/shard_map/ppermute | solution.py:421
  10.0 10.5 %copy-start.1 = (f32[96,256]{1,0:T(8,128)}, f32[96,256]{1,0:T(8,128)S(1)}, u32[]{:S(2)}) copy-start(f32[96,256]{1,0:T(8,128)S(1)} %collective-permute-done.3.refs_4_) | copy-start | bytes 294916
  10.0 5.9 %collective-permute-start.5 = (f32[96,256]{1,0:T(8,128)S(1)}, f32[96,256]{1,0:T(8,128)S(1)}, u32[]{:S(2)}, u32[]{:S(2)}) collective-permute-start(f32[96,256]{1,0:T(8,128)S(1)} %collective-permute-done.3.refs_4_), channel_id=1, source_target_pairs={{0,6},{1,7},{2,4},{3,5},{4,2},{5,3},{6,0},{7,1},{8,14},{9,15},{10,... | collective-permute-start | bytes 294920 | tf_op jit(solution)/shard_map/ppermute | solution.py:421
  11.4 9.2 %copy-start.2 = (f32[96,256]{1,0:T(8,128)}, f32[96,256]{1,0:T(8,128)S(1)}, u32[]{:S(2)}) copy-start(f32[96,256]{1,0:T(8,128)S(1)} %collective-permute-done.6.refs_7_) | copy-start | bytes 294916
  11.4 5.4 %collective-permute-start.7 = (f32[96,256]{1,0:T(8,128)S(1)}, f32[96,256]{1,0:T(8,128)S(1)}, u32[]{:S(2)}, u32[]{:S(2)}) collective-permute-start(f32[96,256]{1,0:T(8,128)S(1)} %collective-permute-done.3.refs_4_), channel_id=1, source_target_pairs={{0,1},{1,0},{2,3},{3,2},{4,5},{5,4},{6,7},{7,6},{8,9},{9,8},{10,11... | collective-permute-start | bytes 294920 | tf_op jit(solution)/shard_map/ppermute | solution.py:421
  11.5 9.1 %copy-start.3 = (f32[96,256]{1,0:T(8,128)}, f32[96,256]{1,0:T(8,128)S(1)}, u32[]{:S(2)}) copy-start(f32[96,256]{1,0:T(8,128)S(1)} %collective-permute-done.4.refs_5_) | copy-start | bytes 294916
  11.5 5.2 %collective-permute-start.8 = (f32[96,256]{1,0:T(8,128)S(1)}, f32[96,256]{1,0:T(8,128)S(1)}, u32[]{:S(2)}, u32[]{:S(2)}) collective-permute-start(f32[96,256]{1,0:T(8,128)S(1)} %collective-permute-done.4.refs_5_), channel_id=1, source_target_pairs={{0,1},{1,0},{2,3},{3,2},{4,5},{5,4},{6,7},{7,6},{8,9},{9,8},{10,11... | collective-permute-start | bytes 294920 | tf_op jit(solution)/shard_map/ppermute | solution.py:421
  14.7 5.9 %copy-start.5 = (f32[96,256]{1,0:T(8,128)}, f32[96,256]{1,0:T(8,128)S(1)}, u32[]{:S(2)}) copy-start(f32[96,256]{1,0:T(8,128)S(1)} %collective-permute-done.refs_1_) | copy-start | bytes 294916
  14.7 5.8 %collective-permute-start.2 = (f32[96,256]{1,0:T(8,128)S(1)}, f32[96,256]{1,0:T(8,128)S(1)}, u32[]{:S(2)}, u32[]{:S(2)}) collective-permute-start(f32[96,256]{1,0:T(8,128)S(1)} %collective-permute-done.refs_1_), channel_id=1, source_target_pairs={{0,24},{1,25},{2,26},{3,27},{4,28},{5,29},{6,30},{7,31},{8,16},{9,... | collective-permute-start | bytes 294920 | tf_op jit(solution)/shard_map/ppermute | solution.py:421
  16.0 4.6 %copy-start.6 = (f32[96,256]{1,0:T(8,128)}, f32[96,256]{1,0:T(8,128)S(1)}, u32[]{:S(2)}) copy-start(f32[96,256]{1,0:T(8,128)S(1)} %collective-permute-done.5.refs_6_) | copy-start | bytes 294916
  16.0 4.5 %collective-permute-start.9 = (f32[96,256]{1,0:T(8,128)S(1)}, f32[96,256]{1,0:T(8,128)S(1)}, u32[]{:S(2)}, u32[]{:S(2)}) collective-permute-start(f32[96,256]{1,0:T(8,128)S(1)} %collective-permute-done.5.refs_6_), channel_id=1, source_target_pairs={{0,1},{1,0},{2,3},{3,2},{4,5},{5,4},{6,7},{7,6},{8,9},{9,8},{10,11... | collective-permute-start | bytes 294920 | tf_op jit(solution)/shard_map/ppermute | solution.py:421
  16.7 3.9 %copy-start.8 = (f32[96,256]{1,0:T(8,128)}, f32[96,256]{1,0:T(8,128)S(1)}, u32[]{:S(2)}) copy-start(f32[96,256]{1,0:T(8,128)S(1)} %collective-permute-done.8.refs_9_) | copy-start | bytes 294916
  212.2 20.8 %collective-permute-start.12 = (f32[64,256]{1,0:T(8,128)}, f32[64,256]{1,0:T(8,128)S(1)}, u32[]{:S(2)}, u32[]{:S(2)}) collective-permute-start(f32[64,256]{1,0:T(8,128)} %get-tuple-element.16), channel_id=1, source_target_pairs={{0,1},{1,0},{2,3},{3,2},{4,5},{5,4},{6,7},{7,6},{8,9},{9,8},{10,11... | collective-permute-start | bytes 196616 | tf_op jit(solution)/shard_map/ppermute | solution.py:421
  218.0 17.2 %collective-permute-start.10 = (f32[32,256]{1,0:T(8,128)}, f32[32,256]{1,0:T(8,128)S(1)}, u32[]{:S(2)}, u32[]{:S(2)}) collective-permute-start(f32[32,256]{1,0:T(8,128)} %get-tuple-element.13), channel_id=1, source_target_pairs={{0,24},{1,25},{2,26},{3,27},{4,28},{5,29},{6,30},{7,31},{8,16},{9,... | collective-permute-start | bytes 98312 | tf_op jit(solution)/shard_map/ppermute | solution.py:421
  233.8 5.1 %collective-permute-start.13 = (f32[32,256]{1,0:T(8,128)S(1)}, f32[32,256]{1,0:T(8,128)S(1)}, u32[]{:S(2)}, u32[]{:S(2)}) collective-permute-start(f32[32,256]{1,0:T(8,128)S(1)} %slice_add_fusion), channel_id=1, source_target_pairs={{0,6},{1,7},{2,4},{3,5},{4,2},{5,3},{6,0},{7,1},{8,14},{9,15},{10,... | collective-permute-start | bytes 98312 | tf_op jit(solution)/shard_map/ppermute | solution.py:421
  235.2 10.0 %collective-permute-start.11 = (f32[16,256]{1,0:T(8,128)S(1)}, f32[16,256]{1,0:T(8,128)S(1)}, u32[]{:S(2)}, u32[]{:S(2)}) collective-permute-start(f32[16,256]{1,0:T(8,128)S(1)} %slice_add_fusion.5), channel_id=1, source_target_pairs={{0,8},{1,9},{2,10},{3,11},{4,12},{5,13},{6,14},{7,15},{8,0},{9,1},... | collective-permute-start | bytes 49160 | tf_op jit(solution)/shard_map/ppermute | solution.py:421
  238.9 8.0 %copy-start.14 = (f32[16,256]{1,0:T(8,128)S(1)}, f32[16,256]{1,0:T(8,128)}, u32[]{:S(2)}) copy-start(f32[16,256]{1,0:T(8,128)} %get-tuple-element.15) | copy-start | bytes 49156
  238.9 8.0 %copy-start.15 = (f32[16,256]{1,0:T(8,128)S(1)}, f32[16,256]{1,0:T(8,128)}, u32[]{:S(2)}) copy-start(f32[16,256]{1,0:T(8,128)} %get-tuple-element.12) | copy-start | bytes 49156
  238.9 8.0 %collective-permute-start.14 = (f32[16,256]{1,0:T(8,128)S(1)}, f32[16,256]{1,0:T(8,128)S(1)}, u32[]{:S(2)}, u32[]{:S(2)}) collective-permute-start(f32[16,256]{1,0:T(8,128)S(1)} %slice_add_fusion.1), channel_id=1, source_target_pairs={{0,2},{1,3},{2,0},{3,1},{4,6},{5,7},{6,4},{7,5},{8,10},{9,11},{10,... | collective-permute-start | bytes 49160 | tf_op jit(solution)/shard_map/ppermute | solution.py:421
  (8 other events, 17.8 us)

commit v3 on v2

--- a/solution.py
+++ b/solution.py
@@ -16,7 +16,10 @@
 CPF = AUX // CHUNK
 WIDE = 4
 NARROW = 8
-SPAN = 64
+SPAN = 96
+WIDE_ROWS = 24
+THIN_ROWS = 16
+LIST_ROWS = WIDE_ROWS + THIN_ROWS
 DUMMY = NF * CPF
 DEPTH = 48
 BATCH = 16
@@ -72,7 +75,7 @@
                 lhs[pl.ds((i * 16 + lf) * CPF + 4 * h, 4)] = feats.astype(jnp.bfloat16).reshape(4, CHUNK, 128)
             return 0
 
-        lax.fori_loop(0, 16, one_row, 0, unroll=4)
+        lax.fori_loop(0, 16, one_row, 0, unroll=16)
     spare_lane = lax.broadcasted_iota(jnp.int32, (CHUNK, 128), 1)
     lhs[DUMMY] = (spare_lane == 4).astype(jnp.float32).astype(jnp.bfloat16)
 
@@ -88,7 +91,7 @@
         rows_s[pl.ds(f * CPF, CPF)] = jnp.zeros((CPF, CHUNK, 128), jnp.float32)
         return 0
 
-    lax.fori_loop(0, NF, one_spread, 0, unroll=4)
+    lax.fori_loop(0, NF, one_spread, 0, unroll=16)
     rows_c[DUMMY] = jnp.zeros((CHUNK, 128), jnp.float32)
     rows_s[DUMMY] = jnp.zeros((CHUNK, 128), jnp.float32)
 
@@ -114,7 +117,7 @@
             rhs[pl.ds(start, 16), :] = jnp.concatenate([take_rows(h, lg, 16) for h in range(2)], axis=1).astype(jnp.bfloat16)
             return 0
 
-        lax.fori_loop(0, 16, one_column, 0, unroll=8)
+        lax.fori_loop(0, 16, one_column, 0, unroll=16)
 
     lane = lax.broadcasted_iota(jnp.int32, (8, AUX), 1)
     back = jnp.zeros((8, AUX), jnp.float32)
@@ -275,31 +278,33 @@
         tiles_thin = tiles - tiles_wide
         for k, tiles in enumerate((tiles_wide, tiles_thin)):
             ends[k] = lax.dot_general(upto, jnp.concatenate([tiles] * 16, axis=0).astype(jnp.bfloat16), contract, preferred_element_type=jnp.float32)
-        number = [(lane8 + 128 * row8 + 1024 * k).astype(jnp.float32) for k in range(2)]
+        number = [(lane8 + 128 * row8 + 1024 * k).astype(jnp.float32) for k in range(WIDE_ROWS // 8)]
+        kinds = [(0, k) for k in range(WIDE_ROWS // 8)] + [(1, k) for k in range(THIN_ROWS // 8)]
 
         def seek(c, state):
             out = []
             column = (c + 1).astype(jnp.float32)
-            for k, (where, begin) in enumerate(state):
-                end = jnp.broadcast_to(ends.at[k // 2][pl.ds(c, 1), :], (8, 128))
-                hit = number[k % 2] >= end
+            edges = [jnp.broadcast_to(ends.at[n][pl.ds(c, 1), :], (8, 128)) for n in range(2)]
+            for (thin, k), (where, begin) in zip(kinds, state):
+                end = edges[thin]
+                hit = number[k] >= end
                 out.append((jnp.where(hit, column, where), jnp.where(hit, end, begin)))
             return tuple(out)
 
-        found = lax.fori_loop(0, NG, seek, ((flat, flat),) * 3, unroll=8)
-        for k, (where, begin) in enumerate(found):
-            place = (number[k % 2] - begin) * (1.0 if k < 2 else 2.0) * 128.0 + where
+        found = lax.fori_loop(0, NG, seek, ((flat, flat),) * len(kinds), unroll=16)
+        for (thin, k), (where, begin) in zip(kinds, found):
+            place = (number[k] - begin) * (128.0 * (1 + thin)) + where
             place = jnp.where(where < float(NG), place, float(groups4 * 128))
-            tiles_v[pl.ds(8 * k, 8), :] = place.astype(jnp.int32)
+            tiles_v[pl.ds(thin * WIDE_ROWS + 8 * k, 8), :] = place.astype(jnp.int32)
         info = jnp.where(row8 == 0, jnp.sum(tiles_wide, axis=1, keepdims=True), jnp.sum(tiles_thin, axis=1, keepdims=True))
-        tiles_v[pl.ds(24, 8), :] = info.astype(jnp.int32)
+        tiles_v[pl.ds(LIST_ROWS, 8), :] = info.astype(jnp.int32)
         longest = jnp.max(total).astype(jnp.int32)
         copies = [pltpu.make_async_copy(table_v, table, sem.at[0]), pltpu.make_async_copy(tiles_v, tile_list, sem.at[1])]
         for copy in copies:
             copy.start()
         for copy in copies:
             copy.wait()
-        count_wide, count_thin = tile_list[24, 0], tile_list[25, 0]
+        count_wide, count_thin = tile_list[LIST_ROWS, 0], tile_list[LIST_ROWS + 1, 0]
 
         def many_tiles(kind, first_row, count):
             take = NARROW if kind == "narrow" else WIDE
@@ -316,7 +321,7 @@
         @pl.when(safe)
         def _():
             many_tiles("wide", 0, count_wide)
-            many_tiles("narrow", 16, count_thin)
+            many_tiles("narrow", WIDE_ROWS, count_thin)
 
         @pl.when(jnp.logical_not(safe))
         def _():
@@ -325,7 +330,7 @@
                 return 0
 
             def thin_one(t, _):
-                exact(tile_list[16 + (t >> 8), (t & 255) >> 1] + 128 * (t & 1))
+                exact(tile_list[WIDE_ROWS + (t >> 8), (t & 255) >> 1] + 128 * (t & 1))
                 return 0
 
             lax.fori_loop(0, count_wide, wide_one, 0)
@@ -348,7 +353,7 @@
             row_sums[h, pl.ds(f, 1), :] = row[0:1, 128 * h:128 * h + 128]
         return 0
 
-    lax.fori_loop(0, NF, collect, 0, unroll=8)
+    lax.fori_loop(0, NF, collect, 0, unroll=16)
     rows_out = jnp.concatenate([row_sums[0], row_sums[1]], axis=1)
     outf_own[...] = rows_out[0:16]
     outf_near[...] = rows_out[16:32]
@@ -389,10 +394,10 @@
             pltpu.VMEM((2, SPAN, 128), jnp.float32),
             pltpu.VMEM((2, 128, 128), jnp.float32),
             pltpu.VMEM((SPAN // WIDE + 2, WIDE, 128), jnp.int32),
-            pltpu.VMEM((32, 128), jnp.int32),
+            pltpu.VMEM((LIST_ROWS + 8, 128), jnp.int32),
             pltpu.VMEM((2, NF, 128), jnp.float32),
             pltpu.SMEM((SPAN // WIDE + 2, WIDE, 128), jnp.int32),
-            pltpu.SMEM((32, 128), jnp.int32),
+            pltpu.SMEM((LIST_ROWS + 8, 128), jnp.int32),
             pltpu.SemaphoreType.DMA((2,)),
         ],
         compiler_params=pltpu.CompilerParams(vmem_limit_bytes=56 * 2**20),

time: 250 us -> 249 us (level); the launches traced: 248 us -> 252 us
  Pallas kernels: 190 us -> 206 us
  starting transfers between devices: 37.4 us -> 26.1 us
    pallas_call x1, Pallas kernels: 190 us -> 206 us  [rectangle(): pl.pallas_call(pair_kernel, out_shape=(shape(64), shape(32), shape(16), s...]
    ppermute x15, starting transfers between devices: 37.4 us -> 26.1 us  [swap(): return lax.ppermute(array, 'frag', pairs)]
where the time goes in v3:
time: 249 us; the launch traced here: 252 us
  Pallas kernels  206 us (83%)
  starting transfers between devices  26.1 us (10%)
  waiting for transfers between devices  13.1 us (5%)
  other arithmetic  3.81 us (2%)
  local copies, waits for them, and re-layouts  2.52 us (1%)
    pallas_call x1, Pallas kernels, rectangle(): pl.pallas_call(pair_kernel, out_shape=(shape(64), shape(32), shape(16), s...  206 us
    ppermute x15, starting transfers between devices, swap(): return lax.ppermute(array, 'frag', pairs)  26.1 us
    ppermute x15, waiting for transfers between devices, swap(): return lax.ppermute(array, 'frag', pairs)  13.1 us
  transfers between devices with their start and end apart: 15, of which 6 were waited for; matrix products, arithmetic and copies ran while one was open for 1% of the time, Pallas kernels for 0%

profile of v3, /device:TPU:0, one launch (start us, length us, event | category | flops | bytes accessed | tf_op | source)
XLA Modules:
  0.0 251.8 jit_solution(2457096873902645919)
XLA Ops:
  0.0 0.7 convert_bitcast_fusion.1
  0.7 0.7 convert_bitcast_fusion
  1.4 0.8 fusion.4
  2.2 1.7 collective-permute-start.3
  3.9 2.1 collective-permute-start.4
  6.0 4.0 %collective-permute-start.1 = (f32[96,256]{1,0:T(8,128)S(1)}, f32[96,256]{1,0:T(8,128)S(1)}, u32[]{:S(2)}, u32[]{:S(2)}) collective-permute-start(f32[96,256]{1,0:T(8,128)S(1)} %select_maximum_fusion.refs_0_), channel_id=1, source_target_pairs={{0,24},{1,25},{2,26},{3,27},{4,28},{5,29},{6,30},{7,31},{8,16},{9,... | collective-permute-start | bytes 294920 | tf_op jit(solution)/shard_map/ppermute | solution.py:426
  10.0 1.2 collective-permute-start.5
  11.5 0.5 collective-permute-start.8
  12.0 2.7 %collective-permute-done.refs_1_ = f32[96,256]{1,0:T(8,128)S(1)} collective-permute-done((f32[96,256]{1,0:T(8,128)S(1)}, f32[96,256]{1,0:T(8,128)S(1)}, u32[]{:S(2)}, u32[]{:S(2)}) %collective-permute-start) | collective-permute-done | bytes 98336 | tf_op jit(solution)/shard_map/ppermute | solution.py:426
  14.7 0.3 collective-permute-start.2
  15.0 1.0 collective-permute-done.5.refs_6_
  16.1 0.6 concatenate.7.meta
  16.7 3.8 %collective-permute-done.2.refs_3_ = f32[96,256]{1,0:T(8,128)S(1)} collective-permute-done((f32[96,256]{1,0:T(8,128)S(1)}, f32[96,256]{1,0:T(8,128)S(1)}, u32[]{:S(2)}, u32[]{:S(2)}) %collective-permute-start.2) | collective-permute-done | bytes 98336 | tf_op jit(solution)/shard_map/ppermute | solution.py:426
  20.6 0.5 copy-done.9
  21.1 0.6 copy-done.10
  21.8 206.2 %shard_map.46 = (f32[64,256]{1,0:T(8,128)}, f32[32,256]{1,0:T(8,128)}, f32[16,256]{1,0:T(8,128)}, f32[16,256]{1,0:T(8,128)}, f32[32,256]{1,0:T(8,128)}, /*index=5*/f32[16,256]{1,0:T(8,128)}, f32[16,256]{1,0:T(8,128)}) custom-call(s32[20]{0:T(128)} %concatenate.7.meta, f32[96,256]{1,0:T(8,128)} %copy-done, f32[96,256]{1,0:T(8,128)} %copy-done.5, ...), custom_call_target="tpu_custom_call" | custom-call | tf_op jit(solution)/shard_map/pallas_call | solution.py:377
  228.0 3.1 %collective-permute-start.10 = (f32[32,256]{1,0:T(8,128)}, f32[32,256]{1,0:T(8,128)S(1)}, u32[]{:S(2)}, u32[]{:S(2)}) collective-permute-start(f32[32,256]{1,0:T(8,128)} %get-tuple-element.13), channel_id=1, source_target_pairs={{0,24},{1,25},{2,26},{3,27},{4,28},{5,29},{6,30},{7,31},{8,16},{9,... | collective-permute-start | bytes 98312 | tf_op jit(solution)/shard_map/ppermute | solution.py:426
  231.2 0.8 slice_add_fusion
  232.0 12.8 %collective-permute-start.13 = (f32[32,256]{1,0:T(8,128)S(1)}, f32[32,256]{1,0:T(8,128)S(1)}, u32[]{:S(2)}, u32[]{:S(2)}) collective-permute-start(f32[32,256]{1,0:T(8,128)S(1)} %slice_add_fusion), channel_id=1, source_target_pairs={{0,6},{1,7},{2,4},{3,5},{4,2},{5,3},{6,0},{7,1},{8,14},{9,15},{10,... | collective-permute-start | bytes 98312 | tf_op jit(solution)/shard_map/ppermute | solution.py:426
  244.9 1.8 collective-permute-done.13
  246.8 1.8 collective-permute-done.11
  248.6 1.9 collective-permute-done.14
  250.5 0.6 copy-done.16
  251.1 0.7 fusion.1
  (55 shorter events, 0.6 us)
Async XLA Ops:
  2.2 18.3 %copy-start = (f32[96,256]{1,0:T(8,128)}, f32[96,256]{1,0:T(8,128)S(1)}, u32[]{:S(2)}) copy-start(f32[96,256]{1,0:T(8,128)S(1)} %select_maximum_fusion.refs_0_) | copy-start | bytes 294916
  2.2 7.8 %collective-permute-start.3 = (f32[96,256]{1,0:T(8,128)S(1)}, f32[96,256]{1,0:T(8,128)S(1)}, u32[]{:S(2)}, u32[]{:S(2)}) collective-permute-start(f32[96,256]{1,0:T(8,128)S(1)} %select_maximum_fusion.refs_0_), channel_id=1, source_target_pairs={{0,2},{1,3},{2,0},{3,1},{4,6},{5,7},{6,4},{7,5},{8,10},{9,11},{10,... | collective-permute-start | bytes 294920 | tf_op jit(solution)/shard_map/ppermute | solution.py:426
  3.9 7.5 %collective-permute-start.6 = (f32[96,256]{1,0:T(8,128)S(1)}, f32[96,256]{1,0:T(8,128)S(1)}, u32[]{:S(2)}, u32[]{:S(2)}) collective-permute-start(f32[96,256]{1,0:T(8,128)S(1)} %select_maximum_fusion.refs_0_), channel_id=1, source_target_pairs={{0,1},{1,0},{2,3},{3,2},{4,5},{5,4},{6,7},{7,6},{8,9},{9,8},{10,11... | collective-permute-start | bytes 294920 | tf_op jit(solution)/shard_map/ppermute | solution.py:426
  3.9 7.5 %collective-permute-start.4 = (f32[96,256]{1,0:T(8,128)S(1)}, f32[96,256]{1,0:T(8,128)S(1)}, u32[]{:S(2)}, u32[]{:S(2)}) collective-permute-start(f32[96,256]{1,0:T(8,128)S(1)} %select_maximum_fusion.refs_0_), channel_id=1, source_target_pairs={{0,6},{1,7},{2,4},{3,5},{4,2},{5,3},{6,0},{7,1},{8,14},{9,15},{10,... | collective-permute-start | bytes 294920 | tf_op jit(solution)/shard_map/ppermute | solution.py:426
  6.0 10.7 %collective-permute-start.1 = (f32[96,256]{1,0:T(8,128)S(1)}, f32[96,256]{1,0:T(8,128)S(1)}, u32[]{:S(2)}, u32[]{:S(2)}) collective-permute-start(f32[96,256]{1,0:T(8,128)S(1)} %select_maximum_fusion.refs_0_), channel_id=1, source_target_pairs={{0,24},{1,25},{2,26},{3,27},{4,28},{5,29},{6,30},{7,31},{8,16},{9,... | collective-permute-start | bytes 294920 | tf_op jit(solution)/shard_map/ppermute | solution.py:426
  10.0 4.6 %collective-permute-start = (f32[96,256]{1,0:T(8,128)S(1)}, f32[96,256]{1,0:T(8,128)S(1)}, u32[]{:S(2)}, u32[]{:S(2)}) collective-permute-start(f32[96,256]{1,0:T(8,128)S(1)} %select_maximum_fusion.refs_0_), channel_id=1, source_target_pairs={{0,8},{1,9},{2,10},{3,11},{4,12},{5,13},{6,14},{7,15},{8,0},{9,1},... | collective-permute-start | bytes 294920 | tf_op jit(solution)/shard_map/ppermute | solution.py:426
  10.0 10.5 %copy-start.1 = (f32[96,256]{1,0:T(8,128)}, f32[96,256]{1,0:T(8,128)S(1)}, u32[]{:S(2)}) copy-start(f32[96,256]{1,0:T(8,128)S(1)} %collective-permute-done.3.refs_4_) | copy-start | bytes 294916
  10.0 5.9 %collective-permute-start.5 = (f32[96,256]{1,0:T(8,128)S(1)}, f32[96,256]{1,0:T(8,128)S(1)}, u32[]{:S(2)}, u32[]{:S(2)}) collective-permute-start(f32[96,256]{1,0:T(8,128)S(1)} %collective-permute-done.3.refs_4_), channel_id=1, source_target_pairs={{0,6},{1,7},{2,4},{3,5},{4,2},{5,3},{6,0},{7,1},{8,14},{9,15},{10,... | collective-permute-start | bytes 294920 | tf_op jit(solution)/shard_map/ppermute | solution.py:426
  11.4 9.2 %copy-start.2 = (f32[96,256]{1,0:T(8,128)}, f32[96,256]{1,0:T(8,128)S(1)}, u32[]{:S(2)}) copy-start(f32[96,256]{1,0:T(8,128)S(1)} %collective-permute-done.6.refs_7_) | copy-start | bytes 294916
  11.4 5.4 %collective-permute-start.7 = (f32[96,256]{1,0:T(8,128)S(1)}, f32[96,256]{1,0:T(8,128)S(1)}, u32[]{:S(2)}, u32[]{:S(2)}) collective-permute-start(f32[96,256]{1,0:T(8,128)S(1)} %collective-permute-done.3.refs_4_), channel_id=1, source_target_pairs={{0,1},{1,0},{2,3},{3,2},{4,5},{5,4},{6,7},{7,6},{8,9},{9,8},{10,11... | collective-permute-start | bytes 294920 | tf_op jit(solution)/shard_map/ppermute | solution.py:426
  11.5 9.1 %copy-start.3 = (f32[96,256]{1,0:T(8,128)}, f32[96,256]{1,0:T(8,128)S(1)}, u32[]{:S(2)}) copy-start(f32[96,256]{1,0:T(8,128)S(1)} %collective-permute-done.4.refs_5_) | copy-start | bytes 294916
  11.5 5.2 %collective-permute-start.8 = (f32[96,256]{1,0:T(8,128)S(1)}, f32[96,256]{1,0:T(8,128)S(1)}, u32[]{:S(2)}, u32[]{:S(2)}) collective-permute-start(f32[96,256]{1,0:T(8,128)S(1)} %collective-permute-done.4.refs_5_), channel_id=1, source_target_pairs={{0,1},{1,0},{2,3},{3,2},{4,5},{5,4},{6,7},{7,6},{8,9},{9,8},{10,11... | collective-permute-start | bytes 294920 | tf_op jit(solution)/shard_map/ppermute | solution.py:426
  14.7 5.9 %copy-start.5 = (f32[96,256]{1,0:T(8,128)}, f32[96,256]{1,0:T(8,128)S(1)}, u32[]{:S(2)}) copy-start(f32[96,256]{1,0:T(8,128)S(1)} %collective-permute-done.refs_1_) | copy-start | bytes 294916
  14.7 5.8 %collective-permute-start.2 = (f32[96,256]{1,0:T(8,128)S(1)}, f32[96,256]{1,0:T(8,128)S(1)}, u32[]{:S(2)}, u32[]{:S(2)}) collective-permute-start(f32[96,256]{1,0:T(8,128)S(1)} %collective-permute-done.refs_1_), channel_id=1, source_target_pairs={{0,24},{1,25},{2,26},{3,27},{4,28},{5,29},{6,30},{7,31},{8,16},{9,... | collective-permute-start | bytes 294920 | tf_op jit(solution)/shard_map/ppermute | solution.py:426
  16.0 4.6 %copy-start.6 = (f32[96,256]{1,0:T(8,128)}, f32[96,256]{1,0:T(8,128)S(1)}, u32[]{:S(2)}) copy-start(f32[96,256]{1,0:T(8,128)S(1)} %collective-permute-done.5.refs_6_) | copy-start | bytes 294916
  16.0 4.5 %collective-permute-start.9 = (f32[96,256]{1,0:T(8,128)S(1)}, f32[96,256]{1,0:T(8,128)S(1)}, u32[]{:S(2)}, u32[]{:S(2)}) collective-permute-start(f32[96,256]{1,0:T(8,128)S(1)} %collective-permute-done.5.refs_6_), channel_id=1, source_target_pairs={{0,1},{1,0},{2,3},{3,2},{4,5},{5,4},{6,7},{7,6},{8,9},{9,8},{10,11... | collective-permute-start | bytes 294920 | tf_op jit(solution)/shard_map/ppermute | solution.py:426
  16.7 3.9 %copy-start.4 = (f32[96,256]{1,0:T(8,128)}, f32[96,256]{1,0:T(8,128)S(1)}, u32[]{:S(2)}) copy-start(f32[96,256]{1,0:T(8,128)S(1)} %collective-permute-done.1.refs_2_) | copy-start | bytes 294916
  16.7 3.9 %copy-start.8 = (f32[96,256]{1,0:T(8,128)}, f32[96,256]{1,0:T(8,128)S(1)}, u32[]{:S(2)}) copy-start(f32[96,256]{1,0:T(8,128)S(1)} %collective-permute-done.8.refs_9_) | copy-start | bytes 294916
  227.9 3.2 %collective-permute-start.12 = (f32[64,256]{1,0:T(8,128)}, f32[64,256]{1,0:T(8,128)S(1)}, u32[]{:S(2)}, u32[]{:S(2)}) collective-permute-start(f32[64,256]{1,0:T(8,128)} %get-tuple-element.16), channel_id=1, source_target_pairs={{0,1},{1,0},{2,3},{3,2},{4,5},{5,4},{6,7},{7,6},{8,9},{9,8},{10,11... | collective-permute-start | bytes 196616 | tf_op jit(solution)/shard_map/ppermute | solution.py:426
  228.0 16.7 %collective-permute-start.10 = (f32[32,256]{1,0:T(8,128)}, f32[32,256]{1,0:T(8,128)S(1)}, u32[]{:S(2)}, u32[]{:S(2)}) collective-permute-start(f32[32,256]{1,0:T(8,128)} %get-tuple-element.13), channel_id=1, source_target_pairs={{0,24},{1,25},{2,26},{3,27},{4,28},{5,29},{6,30},{7,31},{8,16},{9,... | collective-permute-start | bytes 98312 | tf_op jit(solution)/shard_map/ppermute | solution.py:426
  231.2 13.6 %copy-start.12 = (f32[16,256]{1,0:T(8,128)S(1)}, f32[16,256]{1,0:T(8,128)}, u32[]{:S(2)}) copy-start(f32[16,256]{1,0:T(8,128)} %get-tuple-element.14) | copy-start | bytes 49156
  232.0 14.7 %collective-permute-start.13 = (f32[32,256]{1,0:T(8,128)S(1)}, f32[32,256]{1,0:T(8,128)S(1)}, u32[]{:S(2)}, u32[]{:S(2)}) collective-permute-start(f32[32,256]{1,0:T(8,128)S(1)} %slice_add_fusion), channel_id=1, source_target_pairs={{0,6},{1,7},{2,4},{3,5},{4,2},{5,3},{6,0},{7,1},{8,14},{9,15},{10,... | collective-permute-start | bytes 98312 | tf_op jit(solution)/shard_map/ppermute | solution.py:426
  244.8 3.8 %collective-permute-start.11 = (f32[16,256]{1,0:T(8,128)S(1)}, f32[16,256]{1,0:T(8,128)S(1)}, u32[]{:S(2)}, u32[]{:S(2)}) collective-permute-start(f32[16,256]{1,0:T(8,128)S(1)} %slice_add_fusion.5), channel_id=1, source_target_pairs={{0,8},{1,9},{2,10},{3,11},{4,12},{5,13},{6,14},{7,15},{8,0},{9,1},... | collective-permute-start | bytes 49160 | tf_op jit(solution)/shard_map/ppermute | solution.py:426
  246.7 3.8 %collective-permute-start.14 = (f32[16,256]{1,0:T(8,128)S(1)}, f32[16,256]{1,0:T(8,128)S(1)}, u32[]{:S(2)}, u32[]{:S(2)}) collective-permute-start(f32[16,256]{1,0:T(8,128)S(1)} %slice_add_fusion.1), channel_id=1, source_target_pairs={{0,2},{1,3},{2,0},{3,1},{4,6},{5,7},{6,4},{7,5},{8,10},{9,11},{10,... | collective-permute-start | bytes 49160 | tf_op jit(solution)/shard_map/ppermute | solution.py:426
  (8 other events, 17.6 us)
